TPU v7x, 32 devices: a whole 2x2x4 slice. The times are simulated.
32 devices in a mesh: seg: 4 (over y, x), chan: 8 (over z, core).
Axes of the slice: x: 2, y: 2, z: 4, core: 2. Of those that a mesh axis runs over, the one named last changes fastest.
Arguments:
- strain_rate: bfloat16 [48, 256, 4096], P('seg', None, 'chan'), may hold values from -6 to 6
- window_length: int32 [48], P('seg'), may hold values from 1024 to 4096, as said below
- source_channel: int32 [128], replicated, may hold values from 0 to 255, as said below
Outputs:
- stacked: float32 [256, 128, 512], P('chan', 'seg')
Inputs may be any that keep to these rules, and one draw needn't show every extreme that they name: `window_length`: window 0 is fully recorded and window 1 holds exactly 1024 recorded samples. `source_channel`: the virtual sources are distinct channels; channel 0 and the last channel are always among them.
All inputs are finite; a program needn't handle non-finite values.
Results may differ from a plain program's by a relative error of at most 0.0045.
Values may be sent and summed in bfloat16 or wider, within the bound.
No kernel may reach another device: no remote copies, remote signals or barrier semaphores. Data moves between devices by JAX's collectives and lax.ppermute only.
A program may use at most 128 MiB of HBM per device.

v0:
```python
import functools
import itertools
import math

import jax
import jax.numpy as jnp
import ml_dtypes
import numpy as np
from jax import lax
from jax.experimental import pallas as pl
from jax.experimental.pallas import tpu as pltpu
from jax.sharding import PartitionSpec as P

W = 4096
NF = 1152
FIRST_BIN = 16
SMOOTH = 64
MAXLAG = 256
LAGS = 512
RADIX = 8
PART = W // RADIX
TILE = 256
CLASSES = 2
BF16 = jnp.bfloat16
F32 = jnp.float32
VMEM_LIMIT = 60 * 1024 * 1024
GROUPS = ((0,), (4,), (2, 6), (1, 7), (3, 5))
COMPONENTS = ((0, 0), (4, 0), (2, 0), (2, 1), (1, 0), (1, 1), (3, 0), (3, 1))


def phases(first, second):
    product = np.mod(first[:, None].astype(np.int64) * second[None, :], W)
    return product.astype(np.float32) * np.float32(2.0 * math.pi / W)


@functools.lru_cache(maxsize=None)
def bin_order():
    residue = (FIRST_BIN + np.arange(NF)) % RADIX
    return np.concatenate([np.nonzero(residue == r)[0] for group in GROUPS for r in group])


@functools.lru_cache(maxsize=None)
def forward_blocks():
    order = bin_order()
    freqs = FIRST_BIN + order
    residue = freqs % RADIX
    phase = phases(np.arange(PART), freqs)
    cos, sin = np.cos(phase), np.sin(phase)
    base = np.minimum(residue, RADIX - residue)
    sign = np.where(residue == base, 1.0, -1.0).astype(np.float32)
    blocks, layout = [], []
    for begin in range(0, NF, TILE):
        end = min(begin + TILE, NF)
        used = []
        for index, (root, part) in enumerate(COMPONENTS):
            hit = (base[begin:end] == root).astype(np.float32)
            if not hit.any():
                continue
            c, s, g = cos[:, begin:end], sin[:, begin:end], sign[begin:end]
            real = c * hit if part == 0 else g * s * hit
            imag = -s * hit if part == 0 else g * c * hit
            block = np.zeros((PART, 2 * TILE), np.float32)
            block[:, : end - begin] = real
            block[:, TILE : TILE + end - begin] = imag
            used.append((index, len(blocks)))
            blocks.append(block)
        layout.append((begin, end, used))
    return np.stack(blocks).astype(ml_dtypes.bfloat16), layout


@functools.lru_cache(maxsize=None)
def band_tables():
    order = bin_order()
    nearby = np.abs(order[:, None] - order[None, :]) <= SMOOTH
    counts = nearby.sum(axis=0).astype(np.float32)
    return nearby.astype(ml_dtypes.bfloat16), (1.0 / counts)[None, :].astype(np.float32)


@functools.lru_cache(maxsize=None)
def lag_table():
    freqs = FIRST_BIN + bin_order()
    phase = phases(freqs, np.arange(LAGS) - MAXLAG)
    return np.concatenate([np.cos(phase), -np.sin(phase)], axis=0).astype(ml_dtypes.bfloat16)


def pack_kernel(lengths_ref, start_ref, x_ref, out_ref):
    core = lax.rem(pl.program_id(0), 2)
    windows, channels, samples = x_ref.shape
    half = channels // 2
    sample = start_ref[0] + lax.broadcasted_iota(jnp.int32, (half, samples), 1)
    for w in range(windows):
        inside = (sample < lengths_ref[core * windows + w]).astype(F32).astype(BF16)
        for h in range(2):
            out_ref[0, h, w] = x_ref[w, h * half : (h + 1) * half, :] * inside


def pack(strain, lengths, start, chips):
    windows, channels, samples = strain.shape
    per_core = windows // 2
    chip_channels = channels // chips
    return pl.pallas_call(
        pack_kernel,
        grid=(2 * chips,),
        in_specs=[
            pl.BlockSpec(memory_space=pltpu.SMEM),
            pl.BlockSpec(memory_space=pltpu.SMEM),
            pl.BlockSpec((per_core, chip_channels, samples), lambda i: (i % 2, i // 2, 0)),
        ],
        out_specs=pl.BlockSpec(
            (1, 2, per_core, chip_channels // 2, samples), lambda i: (i, 0, 0, 0, 0)
        ),
        out_shape=jax.ShapeDtypeStruct(
            (2 * chips, 2, per_core, chip_channels // 2, samples), BF16
        ),
        compiler_params=pltpu.CompilerParams(vmem_limit_bytes=VMEM_LIMIT),
        name="pack",
    )(lengths, start, strain)


def transform_kernel(layout, core_ref, x_ref, table_ref, nearby_ref, inverse_ref, select_ref,
                     white_ref, own_ref, other_ref, send_ref, spare_ref, parts, real, imag):
    del spare_ref
    slabs, rows, samples = x_ref.shape
    merge = PART // samples
    root = math.sqrt(0.5)
    step = 32

    def fold(i, carry):
        at = pl.ds(pl.multiple_of(i * step, step), step)
        x = []
        for a in range(RADIX):
            pieces = [x_ref[a * merge + j, at, :] for j in range(merge)]
            joined = pieces[0] if merge == 1 else jnp.concatenate(pieces, axis=-1)
            x.append(joined.astype(F32))
        s = [x[a] + x[a + 4] for a in range(4)]
        d = [x[a] - x[a + 4] for a in range(4)]
        even, odd = s[0] + s[2], s[1] + s[3]
        minus, plus = (d[1] - d[3]) * root, (d[1] + d[3]) * root
        values = (
            even + odd, even - odd, s[0] - s[2], s[3] - s[1],
            d[0] + minus, -(d[2] + plus), d[0] - minus, d[2] - plus,
        )
        for index, value in enumerate(values):
            parts[index, at, :] = value.astype(BF16)
        return carry

    lax.fori_loop(0, rows // step, fold, 0)
    for begin, end, used in layout:
        total = None
        for component, block in used:
            term = jnp.dot(parts[component], table_ref[block], preferred_element_type=F32)
            total = term if total is None else total + term
        real[:, begin:end] = total[:, : end - begin]
        imag[:, begin:end] = total[:, TILE : TILE + end - begin]
    re, im = real[...], imag[...]
    magnitude = jnp.sqrt(re * re + im * im).astype(BF16)
    smooth = jnp.dot(magnitude, nearby_ref[...], preferred_element_type=F32)
    inverse = 1.0 / (smooth * inverse_ref[...] + 1e-06)
    white_ref[:, :NF] = (real[...] * inverse).astype(BF16)
    white_ref[:, NF:] = (imag[...] * inverse).astype(BF16)
    half = rows // 2
    core = core_ref[0]
    own_ref[...] = white_ref[pl.ds(pl.multiple_of(core * half, half), half), :]
    other_ref[...] = white_ref[pl.ds(pl.multiple_of((1 - core) * half, half), half), :]
    lanes = send_ref.shape[2]
    for q in range(send_ref.shape[0]):
        chosen = jnp.dot(
            select_ref[q * lanes : (q + 1) * lanes, :], white_ref[...], preferred_element_type=F32
        )
        for begin in range(0, 2 * NF, 128):
            send_ref[q, begin : begin + 128, :] = jnp.transpose(
                chosen[:, begin : begin + 128]
            ).astype(BF16)


def transform(received, select, core, lanes, spare):
    slabs, rows, samples = received.shape
    table, layout = forward_blocks()
    nearby, inverse = band_tables()
    whole = pl.BlockSpec(memory_space=pltpu.VMEM)
    return pl.pallas_call(
        functools.partial(transform_kernel, layout),
        in_specs=[pl.BlockSpec(memory_space=pltpu.SMEM)] + [whole] * 5,
        out_specs=[whole] * 4 + [pl.BlockSpec(memory_space=pl.ANY)],
        out_shape=[
            jax.ShapeDtypeStruct((rows, 2 * NF), BF16),
            jax.ShapeDtypeStruct((rows // 2, 2 * NF), BF16),
            jax.ShapeDtypeStruct((rows // 2, 2 * NF), BF16),
            jax.ShapeDtypeStruct((CLASSES, 2 * NF, lanes), BF16),
            jax.ShapeDtypeStruct(spare, BF16),
        ],
        scratch_shapes=[
            pltpu.VMEM((len(COMPONENTS), rows, PART), BF16),
            pltpu.VMEM((rows, NF), F32),
            pltpu.VMEM((rows, NF), F32),
        ],
        compiler_params=pltpu.CompilerParams(vmem_limit_bytes=VMEM_LIMIT),
        name="transform",
    )(core, received, table, nearby, inverse, select)


def gather_bins_kernel(mine_ref, theirs_ref, out_ref):
    windows, channels, _ = mine_ref.shape
    lane = lax.broadcasted_iota(jnp.int32, (channels, 128), 1)
    upper = [((lane // (8 << bit)) % 2) == 1 for bit in range(4)]

    def turned(tiles):
        tiles = list(tiles)
        for bit in range(4):
            shift = 8 << bit
            for j in range(16):
                if (j >> bit) & 1:
                    continue
                low, high = tiles[j], tiles[j + (1 << bit)]
                if low is None and high is None:
                    continue
                zero = jnp.zeros((channels, 128), F32)
                low = zero if low is None else low
                high = zero if high is None else high
                tiles[j] = jnp.where(upper[bit], pltpu.roll(high, shift, 1), low)
                tiles[j + (1 << bit)] = jnp.where(
                    upper[bit], high, pltpu.roll(low, 128 - shift, 1)
                )
        return tiles

    def tile(i, carry):
        values = []
        for part in range(2):
            at = pl.ds(pl.multiple_of(part * NF + i * 128, 128), 128)
            for ref in (mine_ref, theirs_ref):
                values += [ref[w, :, at].astype(F32) for w in range(windows)]
        first = turned(values[:16])
        second = turned(values[16:] + [None] * (32 - len(values)))
        for g in range(16):
            out_ref[i * 16 + g, :, :128] = first[g]
            out_ref[i * 16 + g, :, 128:] = second[g]
        return carry

    lax.fori_loop(0, NF // 128, tile, 0)


def gather_bins(mine, theirs):
    windows, channels, _ = mine.shape
    whole = pl.BlockSpec(memory_space=pltpu.VMEM)
    return pl.pallas_call(
        gather_bins_kernel,
        in_specs=[whole] * 2,
        out_specs=whole,
        out_shape=jax.ShapeDtypeStruct((NF // 8, channels, TILE), F32),
        compiler_params=pltpu.CompilerParams(vmem_limit_bytes=VMEM_LIMIT),
        name="gather_bins",
    )(mine, theirs)


def correlate_kernel(segs, chunk, full_ref, own_ref, mine_ref, theirs_ref, place_ref, spot_ref,
                     order_ref, table_ref, extra_ref, out_ref, src, cross, spare, sem):
    channels = own_ref.shape[1]
    windows = place_ref.shape[1] // 128
    sources = 64
    low = lax.broadcasted_iota(jnp.int32, (NF, 128), 1) < sources

    def spread(part, values, places):
        for w in range(0, windows, 2):
            at = places[:, w * 128 : (w + 2) * 128]
            re = jnp.dot(values[:NF], at, preferred_element_type=F32)
            im = jnp.dot(values[NF:], at, preferred_element_type=F32)
            for e in range(2):
                r, i = re[:, e * 128 : (e + 1) * 128], im[:, e * 128 : (e + 1) * 128]
                src[part * windows + w + e] = jnp.where(low, r, -i)
                src[(2 + part) * windows + w + e] = jnp.where(low, i, r)

    @pl.when(full_ref[0] == 0)
    def _():
        for part, ref in enumerate((mine_ref, theirs_ref)):
            joined = jnp.concatenate([ref[d] for d in range(ref.shape[0])], axis=1)
            spread(part, joined, place_ref)

    @pl.when(full_ref[0] != 0)
    def _():
        for part in range(2):
            copy = pltpu.make_async_copy(extra_ref.at[chunk, part], spare, sem)
            copy.start()
            copy.wait()
            spread(part, spare[...], spot_ref)

    shape = (8, TILE)
    lane = lax.broadcasted_iota(jnp.int32, shape, 1)
    pick = (lane % 8 == lax.broadcasted_iota(jnp.int32, shape, 0)) & (lane < 32 * windows)
    under = lax.broadcasted_iota(jnp.int32, (16, 128), 1) < sources
    zeros = jnp.zeros((TILE - 32 * windows, 128), F32)

    def bins(i, carry):
        pair = []
        for e in range(2):
            g = 2 * i + e
            at = pl.ds(pl.multiple_of(g * 8, 8), 8)
            right = jnp.concatenate(
                [src[j, at, :] for j in range(4 * windows)] + [zeros], axis=0
            ).astype(BF16)
            own = own_ref[g]
            left = jnp.concatenate(
                [
                    jnp.where(pick, jnp.broadcast_to(own[c : c + 1, :], shape), 0.0)
                    for c in range(channels)
                ],
                axis=0,
            ).astype(BF16)
            pair.append(jnp.dot(left, right, preferred_element_type=F32))
        at = pl.ds(pl.multiple_of(i * 16, 16), 16)
        for c in range(0, channels, 2):
            t = [
                jnp.concatenate([p[(c + e) * 8 : (c + e + 1) * 8] for p in pair], axis=0)
                for e in range(2)
            ]
            re = jnp.where(under, t[0], pltpu.roll(t[1], sources, 1))
            im = jnp.where(under, pltpu.roll(t[0], sources, 1), t[1])
            lanes = slice((c % 4) * 64, (c % 4) * 64 + 128)
            cross[c // 4, 0, at, lanes] = re.astype(BF16)
            cross[c // 4, 1, at, lanes] = im.astype(BF16)
        return carry

    lax.fori_loop(0, NF // 16, bins, 0)

    rows = TILE // segs

    def lags(i, carry):
        lag = jnp.dot(table_ref[0], cross[i, 0], preferred_element_type=F32)
        lag = (lag + jnp.dot(table_ref[1], cross[i, 1], preferred_element_type=F32)).astype(BF16)
        turned = lax.dot_general(
            order_ref[...], lag, (((1,), (1,)), ((), ())), preferred_element_type=F32
        ).astype(BF16)
        at = pl.ds(pl.multiple_of(i * rows, rows), rows)
        for g in range(segs):
            out_ref[g, at, :] = turned[g * rows : (g + 1) * rows, :]
        return carry

    lax.fori_loop(0, channels // 4, lags, 0)


def correlate(chunk, full, own, mine, theirs, place, extra, segs):
    groups, channels, _ = own.shape
    windows = place.shape[1] // 128
    group = 64 // segs
    spot = np.zeros((windows, 64, windows, 2, 64), np.float32)
    for w in range(windows):
        spot[w, :, w] = np.eye(64)[:, None, :]
    spot = spot.reshape(windows * 64, windows * 128).astype(ml_dtypes.bfloat16)
    order = np.zeros((segs, 4, group, 4, segs, group), np.float32)
    for g, c, u in itertools.product(range(segs), range(4), range(group)):
        order[g, c, u, c, g, u] = 1
    order = order.reshape(256, 256).astype(ml_dtypes.bfloat16)
    table = np.ascontiguousarray(lag_table().reshape(2, NF, LAGS).transpose(0, 2, 1))
    whole = pl.BlockSpec(memory_space=pltpu.VMEM)
    return pl.pallas_call(
        functools.partial(correlate_kernel, segs, chunk),
        in_specs=[pl.BlockSpec(memory_space=pltpu.SMEM)]
        + [whole] * 7
        + [pl.BlockSpec(memory_space=pl.ANY)],
        out_specs=whole,
        out_shape=jax.ShapeDtypeStruct((segs, channels * group, LAGS), BF16),
        scratch_shapes=[
            pltpu.VMEM((4 * windows, NF, 128), F32),
            pltpu.VMEM((channels // 4, 2, NF, TILE), BF16),
            pltpu.VMEM(extra.shape[2:], BF16),
            pltpu.SemaphoreType.DMA,
        ],
        compiler_params=pltpu.CompilerParams(vmem_limit_bytes=VMEM_LIMIT),
        name="correlate",
    )(full, own, mine, theirs, place, spot, order, table, extra)


def finish_kernel(scale, place_ref, *refs):
    parts, out_ref = refs[:-1], refs[-1]
    segs = parts[0].shape[0]
    pairs = out_ref.shape[0] // 2
    rows = parts[0].shape[1] // pairs
    block = out_ref.shape[1]
    for i in range(pairs):
        stacked = jnp.concatenate(
            [part[g, i * rows : (i + 1) * rows, :] for g in range(segs) for part in parts], axis=0
        )
        total = jnp.dot(place_ref[...], stacked, preferred_element_type=F32) * scale
        out_ref[2 * i : 2 * i + 2] = total.reshape(2, block, LAGS)


def finish(parts, place, scale, block, channels):
    segs, rows, _ = parts[0].shape
    step = 8
    piece = pl.BlockSpec((segs, rows * step // channels, LAGS), lambda i: (0, i, 0))
    return pl.pallas_call(
        functools.partial(finish_kernel, scale),
        grid=(channels // step,),
        in_specs=[pl.BlockSpec(place.shape, lambda i: (0, 0))] + [piece] * len(parts),
        out_specs=pl.BlockSpec((step, block, LAGS), lambda i: (i, 0, 0)),
        out_shape=jax.ShapeDtypeStruct((channels, block, LAGS), F32),
        compiler_params=pltpu.CompilerParams(vmem_limit_bytes=VMEM_LIMIT),
        name="finish",
    )(place, *parts)


def round_up(value, step):
    return -(-value // step) * step


def plan(source_channel, chips, chip_channels, segs):
    count = source_channel.shape[0]
    block = count // segs
    chip = source_channel // chip_channels
    index = jnp.arange(count, dtype=jnp.int32)
    seg = index // block
    same_seg = seg[:, None] == seg[None, :]
    earlier = index[None, :] < index[:, None]
    same_chip = chip[:, None] == chip[None, :]
    ahead = same_seg & ((chip[None, :] < chip[:, None]) | (same_chip & earlier))
    position = jnp.sum(ahead.astype(jnp.int32), axis=1)
    turns = np.array(
        [(0,) + t for t in itertools.product(range(CLASSES), repeat=segs - 1)], np.int32
    )
    turned = jnp.asarray(np.repeat(turns, block, axis=1))
    classes = (position[None, :] + turned) % CLASSES
    of_class = classes[:, None, :] == jnp.arange(CLASSES, dtype=jnp.int32)[None, :, None]
    of_chip = chip[:, None] == jnp.arange(chips, dtype=jnp.int32)[None, :]
    held = jnp.einsum(
        "rqs,sz->rqz", of_class.astype(BF16), of_chip.astype(BF16), preferred_element_type=F32
    )
    fullest = jnp.max(held, axis=(1, 2))
    best = jnp.argmin(fullest)
    chosen = lax.dynamic_index_in_dim(classes, best, 0, keepdims=False)
    same_class = chosen[:, None] == chosen[None, :]
    place = jnp.sum(
        (same_seg & same_class & (position[None, :] < position[:, None])).astype(jnp.int32), axis=1
    )
    slot = jnp.sum((same_chip & same_class & earlier).astype(jnp.int32), axis=1)
    return chip, chosen, place, slot, seg, jnp.min(fullest)


def on_device(strain_rate, window_length, source_channel):
    chan_index = lax.axis_index("chan")
    seg_index = lax.axis_index("seg")
    devices = lax.axis_size("chan")
    segs = lax.axis_size("seg")
    chips = devices // 2
    windows, all_channels, samples = strain_rate.shape
    channels = all_channels // devices
    per_core = windows // 2
    count = source_channel.shape[0]
    block = count // segs
    group = block // CLASSES
    spots = segs * group
    my_chip = chan_index // 2
    my_core = (chan_index % 2).astype(jnp.int32).reshape(1)

    start = (chan_index * samples).astype(jnp.int32).reshape(1)
    packed = pack(strain_rate, window_length, start, chips)
    packed = packed.reshape(devices, 2 * per_core * channels, samples)
    received = lax.all_to_all(packed, "chan", split_axis=0, concat_axis=0, tiled=True)

    chip, chosen, place, slot, seg, fullest = plan(source_channel, chips, 2 * channels, segs)
    mean = count / CLASSES / chips
    cap = math.ceil(mean + 0.7 * math.sqrt(2 * mean))
    full = (fullest > cap).astype(jnp.int32)

    core_swap = [(i, i ^ 1) for i in range(devices)]
    upward = [(i, i + 2) for i in range(devices - 2)]
    downward = [(i + 2, i) for i in range(devices - 2)]
    lines = [list(range(core, devices, 2)) for core in range(2)]

    row = np.arange(2 * per_core * channels)
    row_window = (row // channels) % per_core
    row_channel = (row // (per_core * channels)) * channels + row % channels
    kinds = jnp.arange(CLASSES, dtype=jnp.int32)
    local = source_channel % (2 * channels)
    here = chip == my_chip

    lanes = round_up(per_core * cap, 128)
    seat = np.arange(lanes)
    seat_window = np.where(seat < per_core * cap, seat // cap, -1).astype(np.int32)
    seat_slot = (seat % cap).astype(np.int32)
    sits = (
        (chosen[None, None, :] == kinds[:, None, None])
        & (slot[None, None, :] == seat_slot[None, :, None])
        & here[None, None, :]
    )
    held = jnp.sum(jnp.where(sits, local[None, None, :] + 1, 0), axis=-1) - 1
    select = (
        (held[:, :, None] == row_channel[None, None, :])
        & (seat_window[:, None] == row_window[None, :])[None]
    ).astype(BF16).reshape(CLASSES * lanes, row.shape[0])

    spot_index = jnp.arange(spots, dtype=jnp.int32)
    at_spot = (
        (chosen[None, None, :] == kinds[:, None, None])
        & (seg * group + place == spot_index[:, None])[None]
    )
    spot_slot = jnp.sum(jnp.where(at_spot, slot[None, None, :], 0), axis=-1)
    spot_chip = jnp.sum(jnp.where(at_spot, chip[None, None, :], 0), axis=-1)
    spot_far = (spot_chip - my_chip) % chips
    column_window = np.repeat(np.arange(per_core), 2 * spots)
    far = np.repeat(np.arange(chips), lanes).astype(np.int32)
    placing = (
        (jnp.tile(spot_slot, (1, 2 * per_core))[:, None, :] == np.tile(seat_slot, chips)[None, :, None])
        & (jnp.tile(spot_far, (1, 2 * per_core))[:, None, :] == far[None, :, None])
        & (np.tile(seat_window, chips)[:, None] == column_window[None, :])[None]
    ).astype(BF16)

    my_chosen = lax.dynamic_slice_in_dim(chosen, seg_index * block, block)
    my_place = lax.dynamic_slice_in_dim(place, seg_index * block, block)
    width = CLASSES * 2 * group
    column = np.arange(segs * width) % width
    row_pair = np.repeat(np.arange(2), block)
    final = (
        (jnp.tile(my_chosen, 2)[:, None] == (column // (2 * group))[None, :])
        & (jnp.tile(my_place, 2)[:, None] == (column % group)[None, :])
        & (row_pair[:, None] == (column // group % 2)[None, :])
    ).astype(BF16)

    spare = (CLASSES, 2, 2 * NF, per_core * spots)
    white, own, other, sends, unused = transform(received, select, my_core, lanes, spare)

    def all_summed(white, unused):
        local_at = jnp.sum(jnp.where(at_spot & here, local[None, None, :] + 1, 0), axis=-1) - 1
        wanted = (
            (jnp.tile(local_at, (1, per_core))[:, :, None] == row_channel[None, None, :])
            & (np.repeat(np.arange(per_core), spots)[:, None] == row_window[None, :])[None]
        ).astype(BF16)
        mine = jnp.einsum("qsr,rk->qks", wanted, white, preferred_element_type=F32).astype(BF16)
        mine = lax.psum(mine, "chan", axis_index_groups=lines)
        theirs = lax.ppermute(mine, "chan", core_swap)
        return jnp.stack([mine, theirs], axis=1)

    extra = lax.cond(full > 0, all_summed, lambda white, unused: unused, white, unused)

    own_other = lax.ppermute(other, "chan", core_swap)
    shape = (per_core, channels, 2 * NF)
    bins = gather_bins(own.reshape(shape), own_other.reshape(shape))

    pieces = []
    for q in range(CLASSES):
        from_below, from_above = [None] * chips, [None] * chips
        up = down = sends[q]
        for hop in range(1, chips):
            up = lax.ppermute(up, "chan", upward)
            down = lax.ppermute(down, "chan", downward)
            from_below[hop], from_above[hop] = up, down
        merged = [sends[q]]
        for far_by in range(1, chips):
            merged.append(from_above[far_by] + from_below[chips - far_by])
        mine = jnp.stack(merged)
        theirs = lax.ppermute(mine, "chan", core_swap)
        lag = correlate(q, full.reshape(1), bins, mine, theirs, placing[q], extra, segs)
        pieces.append(lax.all_to_all(lag, "seg", split_axis=0, concat_axis=0, tiled=True))

    scale = 1.0 / math.sqrt(NF * windows * segs)
    return finish(pieces, final, scale, block, channels)


def solution(mesh):
    in_specs = (P("seg", None, "chan"), P("seg"), P())
    out_specs = P("chan", "seg", None)
    return jax.shard_map(
        on_device, mesh=mesh, in_specs=in_specs, out_specs=out_specs, check_vma=False
    )
```

profile of v0, /device:TPU:0, one launch (start us, length us, event | category | flops | bytes accessed | tf_op | source)
XLA Modules:
  0.0 327.2 jit_solution(10797350030327779619)
XLA Ops:
  6.5 6.2 %pack.1 = bf16[8,2,6,32,512]{4,3,2,1,0:T(8,128)(2,1)} custom-call(s32[12]{0:T(128)} %lengths_ref.1, s32[1]{0:T(128)} %bitcast.9.start_ref, bf16[12,256,512]{2,1,0:T(8,128)(2,1)} %x_ref.1), custom_call_target="tpu_custom_call" | custom-call | tf_op jit(solution)/shard_map/pack/pallas_call | solution.py:101
  12.8 6.5 %all-to-all-start = ((bf16[8,384,512]{2,1,0:T(8,128)(2,1)}), bf16[8,384,512]{2,1,0:T(8,128)(2,1)S(1)}, u32[]{:S(2)}, u32[]{:S(2)}) async-start(bf16[8,384,512]{2,1,0:T(8,128)(2,1)} %bitcast.46), calls=%async_computation | async-start | bytes 6291456 | tf_op jit(solution)/shard_map/all_to_all | solution.py:456
  23.7 67.1 %all-to-all-done.x_ref = bf16[8,384,512]{2,1,0:T(8,128)(2,1)S(1)} async-done(((bf16[8,384,512]{2,1,0:T(8,128)(2,1)}), bf16[8,384,512]{2,1,0:T(8,128)(2,1)S(1)}, u32[]{:S(2)}, u32[]{:S(2)}) %all-to-all-start) | async-done | bytes 3145760 | tf_op jit(solution)/shard_map/all_to_all | solution.py:456
  90.8 1.7 copy-done
  92.5 13.0 %transform.1 = (bf16[384,2304]{1,0:T(8,128)(2,1)}, bf16[192,2304]{1,0:T(8,128)(2,1)}, bf16[192,2304]{1,0:T(8,128)(2,1)}, bf16[2,2304,128]{2,1,0:T(8,128)(2,1)}, bf16[2,2,2304,384]{3,2,1,0:T(8,128)(2,1)}) custom-call(s32[1]{0:T(128)} %bitcast.8.core_ref, bf16[8,384,512]{2,1,0:T(8,128)(2,1)} %copy-done, bf16[15,512,512]{2,1,0:T(8,128)(2,1)} %constant.186.clone.table_ref, ...), custom_call_target="tpu_custom_call" | custom-call | tf_op jit(solution)/shard_map/transform/pallas_call | solution.py:181
  105.5 1.5 fusion.17
  107.1 1.3 collective-permute-start.3
  108.4 1.3 collective-permute-start.2
  109.7 4.6 %collective-permute-start.10 = (bf16[2304,128]{1,0:T(8,128)(2,1)S(1)}, bf16[2304,128]{1,0:T(8,128)(2,1)S(1)}, u32[]{:S(2)}, u32[]{:S(2)}) collective-permute-start(bf16[2304,128]{1,0:T(8,128)(2,1)S(1)} %get-tuple-element.57), channel_id=1, source_target_pairs={{0,2},{1,3},{2,4},{3,5},{4,6},{5,7},{8,10},{9,11},{10,12},{11,13},... | collective-permute-start | bytes 1769480 | tf_op jit(solution)/shard_map/ppermute | solution.py:542
  114.3 1.3 collective-permute-start.9
  115.6 6.5 %collective-permute-done.3 = bf16[2304,128]{1,0:T(8,128)(2,1)S(1)} collective-permute-done((bf16[2304,128]{1,0:T(8,128)(2,1)S(1)}, bf16[2304,128]{1,0:T(8,128)(2,1)S(1)}, u32[]{:S(2)}, u32[]{:S(2)}) %collective-permute-start.3) | collective-permute-done | bytes 589856 | tf_op jit(solution)/shard_map/ppermute | solution.py:542
  122.1 4.4 %collective-permute-start.4 = (bf16[2304,128]{1,0:T(8,128)(2,1)S(1)}, bf16[2304,128]{1,0:T(8,128)(2,1)S(1)}, u32[]{:S(2)}, u32[]{:S(2)}) collective-permute-start(bf16[2304,128]{1,0:T(8,128)(2,1)S(1)} %collective-permute-done.3), channel_id=1, source_target_pairs={{0,2},{1,3},{2,4},{3,5},{4,6},{5,7},{8,10},{9,11},{10,12},{11,13},... | collective-permute-start | bytes 1769480 | tf_op jit(solution)/shard_map/ppermute | solution.py:542
  127.8 6.9 %collective-permute-done.10 = bf16[2304,128]{1,0:T(8,128)(2,1)S(1)} collective-permute-done((bf16[2304,128]{1,0:T(8,128)(2,1)S(1)}, bf16[2304,128]{1,0:T(8,128)(2,1)S(1)}, u32[]{:S(2)}, u32[]{:S(2)}) %collective-permute-start.10) | collective-permute-done | bytes 589856 | tf_op jit(solution)/shard_map/ppermute | solution.py:542
  134.7 4.4 %collective-permute-start.11 = (bf16[2304,128]{1,0:T(8,128)(2,1)S(1)}, bf16[2304,128]{1,0:T(8,128)(2,1)S(1)}, u32[]{:S(2)}, u32[]{:S(2)}) collective-permute-start(bf16[2304,128]{1,0:T(8,128)(2,1)S(1)} %collective-permute-done.10), channel_id=1, source_target_pairs={{0,2},{1,3},{2,4},{3,5},{4,6},{5,7},{8,10},{9,11},{10,12},{11,13},... | collective-permute-start | bytes 1769480 | tf_op jit(solution)/shard_map/ppermute | solution.py:542
  139.4 1.3 collective-permute-start.13
  140.7 6.6 %collective-permute-done.4 = bf16[2304,128]{1,0:T(8,128)(2,1)S(1)} collective-permute-done((bf16[2304,128]{1,0:T(8,128)(2,1)S(1)}, bf16[2304,128]{1,0:T(8,128)(2,1)S(1)}, u32[]{:S(2)}, u32[]{:S(2)}) %collective-permute-start.4) | collective-permute-done | bytes 589856 | tf_op jit(solution)/shard_map/ppermute | solution.py:542
  147.3 4.4 %collective-permute-start.5 = (bf16[2304,128]{1,0:T(8,128)(2,1)S(1)}, bf16[2304,128]{1,0:T(8,128)(2,1)S(1)}, u32[]{:S(2)}, u32[]{:S(2)}) collective-permute-start(bf16[2304,128]{1,0:T(8,128)(2,1)S(1)} %collective-permute-done.4), channel_id=1, source_target_pairs={{0,2},{1,3},{2,4},{3,5},{4,6},{5,7},{8,10},{9,11},{10,12},{11,13},... | collective-permute-start | bytes 1769480 | tf_op jit(solution)/shard_map/ppermute | solution.py:542
  153.1 6.9 %collective-permute-done.11 = bf16[2304,128]{1,0:T(8,128)(2,1)S(1)} collective-permute-done((bf16[2304,128]{1,0:T(8,128)(2,1)S(1)}, bf16[2304,128]{1,0:T(8,128)(2,1)S(1)}, u32[]{:S(2)}, u32[]{:S(2)}) %collective-permute-start.11) | collective-permute-done | bytes 589856 | tf_op jit(solution)/shard_map/ppermute | solution.py:542
  160.0 4.4 %collective-permute-start.12 = (bf16[2304,128]{1,0:T(8,128)(2,1)S(1)}, bf16[2304,128]{1,0:T(8,128)(2,1)S(1)}, u32[]{:S(2)}, u32[]{:S(2)}) collective-permute-start(bf16[2304,128]{1,0:T(8,128)(2,1)S(1)} %collective-permute-done.11), channel_id=1, source_target_pairs={{0,2},{1,3},{2,4},{3,5},{4,6},{5,7},{8,10},{9,11},{10,12},{11,13},... | collective-permute-start | bytes 1769480 | tf_op jit(solution)/shard_map/ppermute | solution.py:542
  165.9 6.8 %collective-permute-done.5 = bf16[2304,128]{1,0:T(8,128)(2,1)S(1)} collective-permute-done((bf16[2304,128]{1,0:T(8,128)(2,1)S(1)}, bf16[2304,128]{1,0:T(8,128)(2,1)S(1)}, u32[]{:S(2)}, u32[]{:S(2)}) %collective-permute-start.5) | collective-permute-done | bytes 589856 | tf_op jit(solution)/shard_map/ppermute | solution.py:542
  172.7 4.4 %collective-permute-done.7 = bf16[2304,128]{1,0:T(8,128)(2,1)S(1)} collective-permute-done((bf16[2304,128]{1,0:T(8,128)(2,1)S(1)}, bf16[2304,128]{1,0:T(8,128)(2,1)S(1)}, u32[]{:S(2)}, u32[]{:S(2)}) %collective-permute-start.7) | collective-permute-done | bytes 589856 | tf_op jit(solution)/shard_map/ppermute | solution.py:543
  177.5 6.7 %collective-permute-done.12 = bf16[2304,128]{1,0:T(8,128)(2,1)S(1)} collective-permute-done((bf16[2304,128]{1,0:T(8,128)(2,1)S(1)}, bf16[2304,128]{1,0:T(8,128)(2,1)S(1)}, u32[]{:S(2)}, u32[]{:S(2)}) %collective-permute-start.12) | collective-permute-done | bytes 589856 | tf_op jit(solution)/shard_map/ppermute | solution.py:542
  184.3 4.1 %collective-permute-done.14 = bf16[2304,128]{1,0:T(8,128)(2,1)S(1)} collective-permute-done((bf16[2304,128]{1,0:T(8,128)(2,1)S(1)}, bf16[2304,128]{1,0:T(8,128)(2,1)S(1)}, u32[]{:S(2)}, u32[]{:S(2)}) %collective-permute-start.14) | collective-permute-done | bytes 589856 | tf_op jit(solution)/shard_map/ppermute | solution.py:543
  188.4 1.7 pad_maximum_fusion.2.mine_ref
  193.0 1.3 slice_bitcast_fusion
  195.2 7.4 %gather_bins.1.own_ref = f32[144,32,256]{2,1,0:T(8,128)} custom-call(bf16[6,32,2304]{2,1,0:T(8,128)(2,1)} %bitcast.49, bf16[6,32,2304]{2,1,0:T(8,128)(2,1)} %bitcast.50), custom_call_target="tpu_custom_call" | custom-call | tf_op jit(solution)/shard_map/gather_bins/pallas_call | solution.py:245
  202.7 39.3 %correlate.2 = bf16[4,512,512]{2,1,0:T(8,128)(2,1)} custom-call(s32[1]{0:T(128)} %bitcast.7.full_ref, f32[144,32,256]{2,1,0:T(8,128)} %gather_bins.1.own_ref, bf16[4,2304,128]{2,1,0:T(8,128)(2,1)} %copy-done.1, bf16[4,2304,128]{2,1,0:T(8,128)(2,1)} %collective-permute-done.8.theirs_ref, bf16[512,768]{1,0:T(8,128)(2,1)} %get-tuple-element.54.place_ref, ...), custom_call_target="tpu_custom_call" | custom-call | tf_op jit(solution)/shard_map/correlate/pallas_call | solution.py:354
  242.0 3.7 %all-to-all-start.1 = ((bf16[4,512,512]{2,1,0:T(8,128)(2,1)}), bf16[4,512,512]{2,1,0:T(8,128)(2,1)S(1)}, u32[]{:S(2)}, u32[]{:S(2)}) async-start(bf16[4,512,512]{2,1,0:T(8,128)(2,1)} %correlate.2), calls=%async_computation.1 | async-start | bytes 4194304 | tf_op jit(solution)/shard_map/all_to_all | solution.py:551
  245.7 39.7 %correlate.3 = bf16[4,512,512]{2,1,0:T(8,128)(2,1)} custom-call(s32[1]{0:T(128)} %bitcast.7.full_ref, f32[144,32,256]{2,1,0:T(8,128)} %gather_bins.1.own_ref, bf16[4,2304,128]{2,1,0:T(8,128)(2,1)} %pad_maximum_fusion.2.mine_ref, bf16[4,2304,128]{2,1,0:T(8,128)(2,1)} %collective-permute-done.15.theirs_ref, bf16[512,768]{1,0:T(8,128)(2,1)} %get-tuple-element.53.place_ref, ...), custom_call_target="tpu_custom_call" | custom-call | tf_op jit(solution)/shard_map/correlate/pallas_call | solution.py:354
  285.4 4.5 %all-to-all-start.2 = ((bf16[4,512,512]{2,1,0:T(8,128)(2,1)}), bf16[4,512,512]{2,1,0:T(8,128)(2,1)}, u32[]{:S(2)}, u32[]{:S(2)}) async-start(bf16[4,512,512]{2,1,0:T(8,128)(2,1)} %correlate.3), calls=%async_computation.2 | async-start | bytes 4194304 | tf_op jit(solution)/shard_map/all_to_all | solution.py:551
  290.9 24.8 %all-to-all-done.2.refs_1_ = bf16[4,512,512]{2,1,0:T(8,128)(2,1)} async-done(((bf16[4,512,512]{2,1,0:T(8,128)(2,1)}), bf16[4,512,512]{2,1,0:T(8,128)(2,1)}, u32[]{:S(2)}, u32[]{:S(2)}) %all-to-all-start.2) | async-done | bytes 2097184 | tf_op jit(solution)/shard_map/all_to_all | solution.py:551
  315.7 4.7 %finish.1 = f32[32,32,512]{2,1,0:T(8,128)} custom-call(bf16[64,256]{1,0:T(8,128)(2,1)} %and_convert_fusion.1.place_ref, bf16[4,512,512]{2,1,0:T(8,128)(2,1)} %copy-done.2, bf16[4,512,512]{2,1,0:T(8,128)(2,1)} %all-to-all-done.2.refs_1_), custom_call_target="tpu_custom_call" | custom-call | tf_op jit(solution)/shard_map/finish/pallas_call | solution.py:390
  (82 shorter events, 11.5 us)
Async XLA Ops:
  12.7 6.5 %copy-start.13 = (s32[128]{0:T(128)S(1)}, s32[128]{0:T(128)}, u32[]{:S(2)}) copy-start(s32[128]{0:T(128)} %param.28) | copy-start | bytes 1540
  12.7 6.7 %copy-start.6 = (s32[8,128]{1,0:T(8,128)S(1)}, s32[8,128]{1,0:T(8,128)}, u32[]{:S(2)}) copy-start(s32[8,128]{1,0:T(8,128)} %constant.176.clone) | copy-start | bytes 12292
  12.7 8.9 %copy-start.4 = (pred[128,384]{1,0:T(32,128)(4,1)S(1)}, pred[128,384]{1,0:T(32,128)(4,1)}, u32[]{:S(2)}) copy-start(pred[128,384]{1,0:T(32,128)(4,1)} %constant.197) | copy-start | bytes 147460
  12.7 9.9 %copy-start.12 = (s32[128]{0:T(128)S(1)}, s32[128]{0:T(128)}, u32[]{:S(2)}) copy-start(s32[128]{0:T(128)} %constant.195) | copy-start | bytes 1540
  12.7 10.1 %copy-start.7 = (s32[384]{0:T(512)S(1)}, s32[384]{0:T(512)}, u32[]{:S(2)}) copy-start(s32[384]{0:T(512)} %constant.196) | copy-start | bytes 4612
  12.8 78.0 %all-to-all-start = ((bf16[8,384,512]{2,1,0:T(8,128)(2,1)}), bf16[8,384,512]{2,1,0:T(8,128)(2,1)S(1)}, u32[]{:S(2)}, u32[]{:S(2)}) async-start(bf16[8,384,512]{2,1,0:T(8,128)(2,1)} %bitcast.46), calls=%async_computation | async-start | bytes 6291456 | tf_op jit(solution)/shard_map/all_to_all | solution.py:456
  90.8 1.7 copy-start
  107.1 15.0 %collective-permute-start.3 = (bf16[2304,128]{1,0:T(8,128)(2,1)S(1)}, bf16[2304,128]{1,0:T(8,128)(2,1)S(1)}, u32[]{:S(2)}, u32[]{:S(2)}) collective-permute-start(bf16[2304,128]{1,0:T(8,128)(2,1)S(1)} %get-tuple-element.56), channel_id=1, source_target_pairs={{0,2},{1,3},{2,4},{3,5},{4,6},{5,7},{8,10},{9,11},{10,12},{11,13},... | collective-permute-start | bytes 1769480 | tf_op jit(solution)/shard_map/ppermute | solution.py:542
  108.4 18.1 %collective-permute-start.2 = (bf16[2304,128]{1,0:T(8,128)(2,1)S(1)}, bf16[2304,128]{1,0:T(8,128)(2,1)S(1)}, u32[]{:S(2)}, u32[]{:S(2)}) collective-permute-start(bf16[2304,128]{1,0:T(8,128)(2,1)S(1)} %get-tuple-element.56), channel_id=1, source_target_pairs={{2,0},{3,1},{4,2},{5,3},{6,4},{7,5},{10,8},{11,9},{12,10},{13,11},... | collective-permute-start | bytes 1769480 | tf_op jit(solution)/shard_map/ppermute | solution.py:543
  109.7 25.0 %collective-permute-start.10 = (bf16[2304,128]{1,0:T(8,128)(2,1)S(1)}, bf16[2304,128]{1,0:T(8,128)(2,1)S(1)}, u32[]{:S(2)}, u32[]{:S(2)}) collective-permute-start(bf16[2304,128]{1,0:T(8,128)(2,1)S(1)} %get-tuple-element.57), channel_id=1, source_target_pairs={{0,2},{1,3},{2,4},{3,5},{4,6},{5,7},{8,10},{9,11},{10,12},{11,13},... | collective-permute-start | bytes 1769480 | tf_op jit(solution)/shard_map/ppermute | solution.py:542
  114.3 25.1 %collective-permute-start.9 = (bf16[2304,128]{1,0:T(8,128)(2,1)S(1)}, bf16[2304,128]{1,0:T(8,128)(2,1)S(1)}, u32[]{:S(2)}, u32[]{:S(2)}) collective-permute-start(bf16[2304,128]{1,0:T(8,128)(2,1)S(1)} %get-tuple-element.57), channel_id=1, source_target_pairs={{2,0},{3,1},{4,2},{5,3},{6,4},{7,5},{10,8},{11,9},{12,10},{13,11},... | collective-permute-start | bytes 1769480 | tf_op jit(solution)/shard_map/ppermute | solution.py:543
  122.1 25.3 %collective-permute-start.4 = (bf16[2304,128]{1,0:T(8,128)(2,1)S(1)}, bf16[2304,128]{1,0:T(8,128)(2,1)S(1)}, u32[]{:S(2)}, u32[]{:S(2)}) collective-permute-start(bf16[2304,128]{1,0:T(8,128)(2,1)S(1)} %collective-permute-done.3), channel_id=1, source_target_pairs={{0,2},{1,3},{2,4},{3,5},{4,6},{5,7},{8,10},{9,11},{10,12},{11,13},... | collective-permute-start | bytes 1769480 | tf_op jit(solution)/shard_map/ppermute | solution.py:542
  126.5 25.3 %collective-permute-start.6 = (bf16[2304,128]{1,0:T(8,128)(2,1)S(1)}, bf16[2304,128]{1,0:T(8,128)(2,1)S(1)}, u32[]{:S(2)}, u32[]{:S(2)}) collective-permute-start(bf16[2304,128]{1,0:T(8,128)(2,1)S(1)} %collective-permute-done.2), channel_id=1, source_target_pairs={{2,0},{3,1},{4,2},{5,3},{6,4},{7,5},{10,8},{11,9},{12,10},{13,11},... | collective-permute-start | bytes 1769480 | tf_op jit(solution)/shard_map/ppermute | solution.py:543
  134.7 25.3 %collective-permute-start.11 = (bf16[2304,128]{1,0:T(8,128)(2,1)S(1)}, bf16[2304,128]{1,0:T(8,128)(2,1)S(1)}, u32[]{:S(2)}, u32[]{:S(2)}) collective-permute-start(bf16[2304,128]{1,0:T(8,128)(2,1)S(1)} %collective-permute-done.10), channel_id=1, source_target_pairs={{0,2},{1,3},{2,4},{3,5},{4,6},{5,7},{8,10},{9,11},{10,12},{11,13},... | collective-permute-start | bytes 1769480 | tf_op jit(solution)/shard_map/ppermute | solution.py:542
  139.3 55.0 %collective-permute-start.1 = (bf16[192,2304]{1,0:T(8,128)(2,1)}, bf16[192,2304]{1,0:T(8,128)(2,1)S(1)}, u32[]{:S(2)}, u32[]{:S(2)}) collective-permute-start(bf16[192,2304]{1,0:T(8,128)(2,1)} %get-tuple-element.38), channel_id=1, source_target_pairs={{0,1},{1,0},{2,3},{3,2},{4,5},{5,4},{6,7},{7,6},{8,9},{9,8},{10,11... | collective-permute-start | bytes 2654216 | tf_op jit(solution)/shard_map/ppermute | solution.py:533
  139.4 25.1 %collective-permute-start.13 = (bf16[2304,128]{1,0:T(8,128)(2,1)S(1)}, bf16[2304,128]{1,0:T(8,128)(2,1)S(1)}, u32[]{:S(2)}, u32[]{:S(2)}) collective-permute-start(bf16[2304,128]{1,0:T(8,128)(2,1)S(1)} %collective-permute-done.9), channel_id=1, source_target_pairs={{2,0},{3,1},{4,2},{5,3},{6,4},{7,5},{10,8},{11,9},{12,10},{13,11},... | collective-permute-start | bytes 1769480 | tf_op jit(solution)/shard_map/ppermute | solution.py:543
  147.3 25.3 %collective-permute-start.5 = (bf16[2304,128]{1,0:T(8,128)(2,1)S(1)}, bf16[2304,128]{1,0:T(8,128)(2,1)S(1)}, u32[]{:S(2)}, u32[]{:S(2)}) collective-permute-start(bf16[2304,128]{1,0:T(8,128)(2,1)S(1)} %collective-permute-done.4), channel_id=1, source_target_pairs={{0,2},{1,3},{2,4},{3,5},{4,6},{5,7},{8,10},{9,11},{10,12},{11,13},... | collective-permute-start | bytes 1769480 | tf_op jit(solution)/shard_map/ppermute | solution.py:542
  151.8 25.3 %collective-permute-start.7 = (bf16[2304,128]{1,0:T(8,128)(2,1)S(1)}, bf16[2304,128]{1,0:T(8,128)(2,1)S(1)}, u32[]{:S(2)}, u32[]{:S(2)}) collective-permute-start(bf16[2304,128]{1,0:T(8,128)(2,1)S(1)} %collective-permute-done.6), channel_id=1, source_target_pairs={{2,0},{3,1},{4,2},{5,3},{6,4},{7,5},{10,8},{11,9},{12,10},{13,11},... | collective-permute-start | bytes 1769480 | tf_op jit(solution)/shard_map/ppermute | solution.py:543
  160.0 24.2 %collective-permute-start.12 = (bf16[2304,128]{1,0:T(8,128)(2,1)S(1)}, bf16[2304,128]{1,0:T(8,128)(2,1)S(1)}, u32[]{:S(2)}, u32[]{:S(2)}) collective-permute-start(bf16[2304,128]{1,0:T(8,128)(2,1)S(1)} %collective-permute-done.11), channel_id=1, source_target_pairs={{0,2},{1,3},{2,4},{3,5},{4,6},{5,7},{8,10},{9,11},{10,12},{11,13},... | collective-permute-start | bytes 1769480 | tf_op jit(solution)/shard_map/ppermute | solution.py:542
  164.5 23.9 %collective-permute-start.14 = (bf16[2304,128]{1,0:T(8,128)(2,1)S(1)}, bf16[2304,128]{1,0:T(8,128)(2,1)S(1)}, u32[]{:S(2)}, u32[]{:S(2)}) collective-permute-start(bf16[2304,128]{1,0:T(8,128)(2,1)S(1)} %collective-permute-done.13), channel_id=1, source_target_pairs={{2,0},{3,1},{4,2},{5,3},{6,4},{7,5},{10,8},{11,9},{12,10},{13,11},... | collective-permute-start | bytes 1769480 | tf_op jit(solution)/shard_map/ppermute | solution.py:543
  177.5 12.7 %copy-start.1 = (bf16[4,2304,128]{2,1,0:T(8,128)(2,1)}, bf16[4,2304,128]{2,1,0:T(8,128)(2,1)S(1)}, u32[]{:S(2)}) copy-start(bf16[4,2304,128]{2,1,0:T(8,128)(2,1)S(1)} %pad_maximum_fusion.1.mine_ref) | copy-start | bytes 7077892
  177.5 25.2 %collective-permute-start.8 = (bf16[4,2304,128]{2,1,0:T(8,128)(2,1)S(1)}, bf16[4,2304,128]{2,1,0:T(8,128)(2,1)}, u32[]{:S(2)}, u32[]{:S(2)}) collective-permute-start(bf16[4,2304,128]{2,1,0:T(8,128)(2,1)S(1)} %pad_maximum_fusion.1.mine_ref), channel_id=1, source_target_pairs={{0,1},{1,0},{2,3},{3,2},{4,5},{5,4},{6,7},{7,6},{8,9},{9,8},{10,11... | collective-permute-start | bytes 7077896 | tf_op jit(solution)/shard_map/ppermute | solution.py:549
  188.4 3.7 %copy-start.8 = (s32[512]{0:T(512)S(1)}, s32[512]{0:T(512)}, u32[]{:S(2)}) copy-start(s32[512]{0:T(512)} %constant.199) | copy-start | bytes 6148
  188.4 3.7 %copy-start.9 = (s32[512]{0:T(512)S(1)}, s32[512]{0:T(512)}, u32[]{:S(2)}) copy-start(s32[512]{0:T(512)} %constant.198) | copy-start | bytes 6148
  190.2 55.5 %collective-permute-start.15 = (bf16[4,2304,128]{2,1,0:T(8,128)(2,1)}, bf16[4,2304,128]{2,1,0:T(8,128)(2,1)}, u32[]{:S(2)}, u32[]{:S(2)}) collective-permute-start(bf16[4,2304,128]{2,1,0:T(8,128)(2,1)} %pad_maximum_fusion.2.mine_ref), channel_id=1, source_target_pairs={{0,1},{1,0},{2,3},{3,2},{4,5},{5,4},{6,7},{7,6},{8,9},{9,8},{10,11... | collective-permute-start | bytes 7077896 | tf_op jit(solution)/shard_map/ppermute | solution.py:549
  194.3 0.9 copy-start.3
  242.0 43.4 %all-to-all-start.1 = ((bf16[4,512,512]{2,1,0:T(8,128)(2,1)}), bf16[4,512,512]{2,1,0:T(8,128)(2,1)S(1)}, u32[]{:S(2)}, u32[]{:S(2)}) async-start(bf16[4,512,512]{2,1,0:T(8,128)(2,1)} %correlate.2), calls=%async_computation.1 | async-start | bytes 4194304 | tf_op jit(solution)/shard_map/all_to_all | solution.py:551
  285.4 4.9 %copy-start.5 = (pred[64,256]{1,0:T(32,128)(4,1)S(1)}, pred[64,256]{1,0:T(32,128)(4,1)}, u32[]{:S(2)}) copy-start(pred[64,256]{1,0:T(32,128)(4,1)} %constant.185.clone) | copy-start | bytes 49156
  285.4 4.9 %copy-start.10 = (s32[256]{0:T(256)S(1)}, s32[256]{0:T(256)}, u32[]{:S(2)}) copy-start(s32[256]{0:T(256)} %constant.194) | copy-start | bytes 3076
  285.4 4.9 %copy-start.11 = (s32[256]{0:T(256)S(1)}, s32[256]{0:T(256)}, u32[]{:S(2)}) copy-start(s32[256]{0:T(256)} %constant.193) | copy-start | bytes 3076
  285.4 30.3 %copy-start.2 = (bf16[4,512,512]{2,1,0:T(8,128)(2,1)}, bf16[4,512,512]{2,1,0:T(8,128)(2,1)S(1)}, u32[]{:S(2)}) copy-start(bf16[4,512,512]{2,1,0:T(8,128)(2,1)S(1)} %all-to-all-done.1.refs_0_) | copy-start | bytes 6291460
  285.4 30.3 %all-to-all-start.2 = ((bf16[4,512,512]{2,1,0:T(8,128)(2,1)}), bf16[4,512,512]{2,1,0:T(8,128)(2,1)}, u32[]{:S(2)}, u32[]{:S(2)}) async-start(bf16[4,512,512]{2,1,0:T(8,128)(2,1)} %correlate.3), calls=%async_computation.2 | async-start | bytes 4194304 | tf_op jit(solution)/shard_map/all_to_all | solution.py:551
where the time goes:
time: 328 us; the launch traced here: 327 us
  waiting for transfers between devices  141 us (43%)
  Pallas kernels  110 us (34%)
  starting transfers between devices  46.1 us (14%)
  between operations  16.4 us (5%)
  local copies, waits for them, and re-layouts  7.23 us (2%)
  other arithmetic  6.28 us (2%)
    pallas_call x2, Pallas kernels, correlate(): pl.pallas_call(functools.partial(correlate_kernel, segs, chunk), in_specs...  79 us
    all_to_all x1, waiting for transfers between devices, on_device(): lax.all_to_all(packed, 'chan', split_axis=0, concat_axis=0, tiled=True)  67.1 us
    ppermute x6, waiting for transfers between devices, on_device(): up = lax.ppermute(up, 'chan', upward)  40.3 us
    all_to_all x2, waiting for transfers between devices, on_device(): lax.all_to_all(lag, 'seg', split_axis=0, concat_axis=0, tiled=True)  24.8 us
    ppermute x6, starting transfers between devices, on_device(): up = lax.ppermute(up, 'chan', upward)  23.6 us
    pallas_call x1, Pallas kernels, transform(): pl.pallas_call(functools.partial(transform_kernel, layout), in_specs=[pl....  13 us
    ppermute x6, waiting for transfers between devices, on_device(): down = lax.ppermute(down, 'chan', downward)  8.61 us
    all_to_all x2, starting transfers between devices, on_device(): lax.all_to_all(lag, 'seg', split_axis=0, concat_axis=0, tiled=True)  8.18 us
  transfers between devices with their start and end apart: 18, of which 12 were waited for; matrix products, arithmetic and copies ran while one was open for 3% of the time, Pallas kernels for 26%

commit v1 on v0

--- a/solution.py
+++ b/solution.py
@@ -118,8 +118,7 @@
 
 
 def transform_kernel(layout, core_ref, x_ref, table_ref, nearby_ref, inverse_ref, select_ref,
-                     white_ref, own_ref, other_ref, send_ref, spare_ref, parts, real, imag):
-    del spare_ref
+                     white_ref, own_ref, other_ref, send_ref, parts, real, imag):
     slabs, rows, samples = x_ref.shape
     merge = PART // samples
     root = math.sqrt(0.5)
@@ -173,7 +172,7 @@
             ).astype(BF16)
 
 
-def transform(received, select, core, lanes, spare):
+def transform(received, select, core, lanes):
     slabs, rows, samples = received.shape
     table, layout = forward_blocks()
     nearby, inverse = band_tables()
@@ -181,13 +180,12 @@
     return pl.pallas_call(
         functools.partial(transform_kernel, layout),
         in_specs=[pl.BlockSpec(memory_space=pltpu.SMEM)] + [whole] * 5,
-        out_specs=[whole] * 4 + [pl.BlockSpec(memory_space=pl.ANY)],
+        out_specs=[whole] * 4,
         out_shape=[
             jax.ShapeDtypeStruct((rows, 2 * NF), BF16),
             jax.ShapeDtypeStruct((rows // 2, 2 * NF), BF16),
             jax.ShapeDtypeStruct((rows // 2, 2 * NF), BF16),
             jax.ShapeDtypeStruct((CLASSES, 2 * NF, lanes), BF16),
-            jax.ShapeDtypeStruct(spare, BF16),
         ],
         scratch_shapes=[
             pltpu.VMEM((len(COMPONENTS), rows, PART), BF16),
@@ -232,8 +230,8 @@
         first = turned(values[:16])
         second = turned(values[16:] + [None] * (32 - len(values)))
         for g in range(16):
-            out_ref[i * 16 + g, :, :128] = first[g]
-            out_ref[i * 16 + g, :, 128:] = second[g]
+            out_ref[i * 16 + g, :, :128] = first[g].astype(BF16)
+            out_ref[i * 16 + g, :, 128:] = second[g].astype(BF16)
         return carry
 
     lax.fori_loop(0, NF // 128, tile, 0)
@@ -246,14 +244,14 @@
         gather_bins_kernel,
         in_specs=[whole] * 2,
         out_specs=whole,
-        out_shape=jax.ShapeDtypeStruct((NF // 8, channels, TILE), F32),
+        out_shape=jax.ShapeDtypeStruct((NF // 8, channels, TILE), BF16),
         compiler_params=pltpu.CompilerParams(vmem_limit_bytes=VMEM_LIMIT),
         name="gather_bins",
     )(mine, theirs)
 
 
-def correlate_kernel(segs, chunk, full_ref, own_ref, mine_ref, theirs_ref, place_ref, spot_ref,
-                     order_ref, table_ref, extra_ref, out_ref, src, cross, spare, sem):
+def correlate_kernel(segs, own_ref, mine_ref, theirs_ref, place_ref, order_ref, table_ref,
+                     out_ref, src, cross):
     channels = own_ref.shape[1]
     windows = place_ref.shape[1] // 128
     sources = 64
@@ -269,19 +267,9 @@
                 src[part * windows + w + e] = jnp.where(low, r, -i)
                 src[(2 + part) * windows + w + e] = jnp.where(low, i, r)
 
-    @pl.when(full_ref[0] == 0)
-    def _():
-        for part, ref in enumerate((mine_ref, theirs_ref)):
-            joined = jnp.concatenate([ref[d] for d in range(ref.shape[0])], axis=1)
-            spread(part, joined, place_ref)
-
-    @pl.when(full_ref[0] != 0)
-    def _():
-        for part in range(2):
-            copy = pltpu.make_async_copy(extra_ref.at[chunk, part], spare, sem)
-            copy.start()
-            copy.wait()
-            spread(part, spare[...], spot_ref)
+    for part, ref in enumerate((mine_ref, theirs_ref)):
+        joined = jnp.concatenate([ref[d] for d in range(ref.shape[0])], axis=1)
+        spread(part, joined, place_ref)
 
     shape = (8, TILE)
     lane = lax.broadcasted_iota(jnp.int32, shape, 1)
@@ -297,7 +285,7 @@
             right = jnp.concatenate(
                 [src[j, at, :] for j in range(4 * windows)] + [zeros], axis=0
             ).astype(BF16)
-            own = own_ref[g]
+            own = own_ref[g].astype(F32)
             left = jnp.concatenate(
                 [
                     jnp.where(pick, jnp.broadcast_to(own[c : c + 1, :], shape), 0.0)
@@ -307,6 +295,7 @@
             ).astype(BF16)
             pair.append(jnp.dot(left, right, preferred_element_type=F32))
         at = pl.ds(pl.multiple_of(i * 16, 16), 16)
+        at_im = pl.ds(pl.multiple_of(NF + i * 16, 16), 16)
         for c in range(0, channels, 2):
             t = [
                 jnp.concatenate([p[(c + e) * 8 : (c + e + 1) * 8] for p in pair], axis=0)
@@ -315,17 +304,16 @@
             re = jnp.where(under, t[0], pltpu.roll(t[1], sources, 1))
             im = jnp.where(under, pltpu.roll(t[0], sources, 1), t[1])
             lanes = slice((c % 4) * 64, (c % 4) * 64 + 128)
-            cross[c // 4, 0, at, lanes] = re.astype(BF16)
-            cross[c // 4, 1, at, lanes] = im.astype(BF16)
+            cross[c // 4, at, lanes] = re.astype(BF16)
+            cross[c // 4, at_im, lanes] = im.astype(BF16)
         return carry
 
-    lax.fori_loop(0, NF // 16, bins, 0)
+    lax.fori_loop(0, NF // 16, bins, 0, unroll=4)
 
     rows = TILE // segs
 
     def lags(i, carry):
-        lag = jnp.dot(table_ref[0], cross[i, 0], preferred_element_type=F32)
-        lag = (lag + jnp.dot(table_ref[1], cross[i, 1], preferred_element_type=F32)).astype(BF16)
+        lag = jnp.dot(table_ref[...], cross[i], preferred_element_type=F32).astype(BF16)
         turned = lax.dot_general(
             order_ref[...], lag, (((1,), (1,)), ((), ())), preferred_element_type=F32
         ).astype(BF16)
@@ -337,36 +325,28 @@
     lax.fori_loop(0, channels // 4, lags, 0)
 
 
-def correlate(chunk, full, own, mine, theirs, place, extra, segs):
+def correlate(own, mine, theirs, place, segs):
     groups, channels, _ = own.shape
     windows = place.shape[1] // 128
     group = 64 // segs
-    spot = np.zeros((windows, 64, windows, 2, 64), np.float32)
-    for w in range(windows):
-        spot[w, :, w] = np.eye(64)[:, None, :]
-    spot = spot.reshape(windows * 64, windows * 128).astype(ml_dtypes.bfloat16)
     order = np.zeros((segs, 4, group, 4, segs, group), np.float32)
     for g, c, u in itertools.product(range(segs), range(4), range(group)):
         order[g, c, u, c, g, u] = 1
     order = order.reshape(256, 256).astype(ml_dtypes.bfloat16)
-    table = np.ascontiguousarray(lag_table().reshape(2, NF, LAGS).transpose(0, 2, 1))
+    table = np.ascontiguousarray(lag_table().T)
     whole = pl.BlockSpec(memory_space=pltpu.VMEM)
     return pl.pallas_call(
-        functools.partial(correlate_kernel, segs, chunk),
-        in_specs=[pl.BlockSpec(memory_space=pltpu.SMEM)]
-        + [whole] * 7
-        + [pl.BlockSpec(memory_space=pl.ANY)],
+        functools.partial(correlate_kernel, segs),
+        in_specs=[whole] * 6,
         out_specs=whole,
         out_shape=jax.ShapeDtypeStruct((segs, channels * group, LAGS), BF16),
         scratch_shapes=[
             pltpu.VMEM((4 * windows, NF, 128), F32),
-            pltpu.VMEM((channels // 4, 2, NF, TILE), BF16),
-            pltpu.VMEM(extra.shape[2:], BF16),
-            pltpu.SemaphoreType.DMA,
+            pltpu.VMEM((channels // 4, 2 * NF, TILE), BF16),
         ],
         compiler_params=pltpu.CompilerParams(vmem_limit_bytes=VMEM_LIMIT),
         name="correlate",
-    )(full, own, mine, theirs, place, spot, order, table, extra)
+    )(own, mine, theirs, place, order, table)
 
 
 def finish_kernel(scale, place_ref, *refs):
@@ -456,8 +436,8 @@
     received = lax.all_to_all(packed, "chan", split_axis=0, concat_axis=0, tiled=True)
 
     chip, chosen, place, slot, seg, fullest = plan(source_channel, chips, 2 * channels, segs)
-    mean = count / CLASSES / chips
-    cap = math.ceil(mean + 0.7 * math.sqrt(2 * mean))
+    lanes = round_up(per_core * -(-count // (CLASSES * chips)), 128)
+    cap = lanes // per_core
     full = (fullest > cap).astype(jnp.int32)
 
     core_swap = [(i, i ^ 1) for i in range(devices)]
@@ -472,7 +452,6 @@
     local = source_channel % (2 * channels)
     here = chip == my_chip
 
-    lanes = round_up(per_core * cap, 128)
     seat = np.arange(lanes)
     seat_window = np.where(seat < per_core * cap, seat // cap, -1).astype(np.int32)
     seat_slot = (seat % cap).astype(np.int32)
@@ -494,7 +473,7 @@
     )
     spot_slot = jnp.sum(jnp.where(at_spot, slot[None, None, :], 0), axis=-1)
     spot_chip = jnp.sum(jnp.where(at_spot, chip[None, None, :], 0), axis=-1)
-    spot_far = (spot_chip - my_chip) % chips
+    spot_far = jnp.stack([(spot_chip[0] - my_chip) % chips, spot_chip[1]])
     column_window = np.repeat(np.arange(per_core), 2 * spots)
     far = np.repeat(np.arange(chips), lanes).astype(np.int32)
     placing = (
@@ -514,44 +493,65 @@
         & (row_pair[:, None] == (column // group % 2)[None, :])
     ).astype(BF16)
 
-    spare = (CLASSES, 2, 2 * NF, per_core * spots)
-    white, own, other, sends, unused = transform(received, select, my_core, lanes, spare)
-
-    def all_summed(white, unused):
-        local_at = jnp.sum(jnp.where(at_spot & here, local[None, None, :] + 1, 0), axis=-1) - 1
-        wanted = (
-            (jnp.tile(local_at, (1, per_core))[:, :, None] == row_channel[None, None, :])
-            & (np.repeat(np.arange(per_core), spots)[:, None] == row_window[None, :])[None]
-        ).astype(BF16)
-        mine = jnp.einsum("qsr,rk->qks", wanted, white, preferred_element_type=F32).astype(BF16)
-        mine = lax.psum(mine, "chan", axis_index_groups=lines)
-        theirs = lax.ppermute(mine, "chan", core_swap)
-        return jnp.stack([mine, theirs], axis=1)
-
-    extra = lax.cond(full > 0, all_summed, lambda white, unused: unused, white, unused)
-
+    white, own, other, sends = transform(received, select, my_core, lanes)
     own_other = lax.ppermute(other, "chan", core_swap)
     shape = (per_core, channels, 2 * NF)
     bins = gather_bins(own.reshape(shape), own_other.reshape(shape))
 
-    pieces = []
-    for q in range(CLASSES):
-        from_below, from_above = [None] * chips, [None] * chips
-        up = down = sends[q]
-        for hop in range(1, chips):
-            up = lax.ppermute(up, "chan", upward)
-            down = lax.ppermute(down, "chan", downward)
-            from_below[hop], from_above[hop] = up, down
-        merged = [sends[q]]
-        for far_by in range(1, chips):
-            merged.append(from_above[far_by] + from_below[chips - far_by])
-        mine = jnp.stack(merged)
+    from_below, from_above = [None] * chips, [None] * chips
+    up = down = sends[0]
+    for hop in range(1, chips):
+        up = lax.ppermute(up, "chan", upward)
+        down = lax.ppermute(down, "chan", downward)
+        if hop == 2:
+            up, down, bins, second = lax.optimization_barrier((up, down, bins, sends[1]))
+        from_below[hop], from_above[hop] = up, down
+    second = lax.all_gather(second, "chan", axis_index_groups=lines)
+    merged = [sends[0]]
+    for far_by in range(1, chips):
+        merged.append(from_above[far_by] + from_below[chips - far_by])
+
+    def stacks(mine, places):
         theirs = lax.ppermute(mine, "chan", core_swap)
-        lag = correlate(q, full.reshape(1), bins, mine, theirs, placing[q], extra, segs)
-        pieces.append(lax.all_to_all(lag, "seg", split_axis=0, concat_axis=0, tiled=True))
+        return correlate(bins, mine, theirs, places, segs)
 
     scale = 1.0 / math.sqrt(NF * windows * segs)
-    return finish(pieces, final, scale, block, channels)
+
+    def finished(lags):
+        pieces = [
+            lax.all_to_all(lag, "seg", split_axis=0, concat_axis=0, tiled=True) for lag in lags
+        ]
+        return finish(pieces, final, scale, block, channels)
+
+    first_lag = stacks(jnp.stack(merged), placing[0])
+    first_lag, second = lax.optimization_barrier((first_lag, second))
+    second_lag = stacks(second, placing[1])
+    seated = finished([first_lag, second_lag])
+
+    def add_unseated(total):
+        out = slot >= cap
+        at = jnp.sum(jnp.where(at_spot & here & out, local[None, None, :] + 1, 0), axis=-1) - 1
+        wanted = (
+            (jnp.tile(at, (1, per_core))[:, :, None] == row_channel[None, None, :])
+            & (np.repeat(np.arange(per_core), spots)[:, None] == row_window[None, :])[None]
+        ).astype(BF16)
+        spot = np.zeros((per_core, spots, per_core, 2, spots), np.float32)
+        for w in range(per_core):
+            spot[w, :, w] = np.eye(spots)[:, None, :]
+        spot = jnp.asarray(spot.reshape(per_core * spots, -1), BF16)
+        lags = []
+        for q in range(CLASSES):
+            mine = jnp.einsum("sr,rk->ks", wanted[q], white, preferred_element_type=F32)
+            mine = lax.psum(mine.astype(BF16), "chan", axis_index_groups=lines)
+            lags.append(stacks(mine[None], spot))
+        return total + finished(lags)
+
+    _, stacked = lax.while_loop(
+        lambda carry: carry[0] < full,
+        lambda carry: (carry[0] + 1, add_unseated(carry[1])),
+        (jnp.zeros((), jnp.int32), seated),
+    )
+    return stacked
 
 
 def solution(mesh):

time: 328 us -> 278 us (0.85)
  Pallas kernels: 110 us -> 81 us
  starting transfers between devices: 46.1 us -> 29.8 us
  waiting for transfers between devices: 141 us -> 134 us
  other arithmetic: 6.28 us -> 10 us
    pallas_call x2, Pallas kernels: 79 us -> 51.8 us  [correlate(): pl.pallas_call(functools.partial(correlate_kernel, segs), in_specs=[whole...]
    ppermute x6 -> x3, waiting for transfers between devices: 40.3 us -> 22.5 us  [on_device(): up = lax.ppermute(up, 'chan', upward)]
    ppermute x6 -> x3, starting transfers between devices: 23.6 us -> 10.1 us  [on_device(): up = lax.ppermute(up, 'chan', upward)]
    ppermute x6 -> x3, waiting for transfers between devices: 8.61 us -> 18.5 us  [on_device(): down = lax.ppermute(down, 'chan', downward)]
    ppermute x6 -> x3, starting transfers between devices: 7.73 us -> 4.03 us  [on_device(): down = lax.ppermute(down, 'chan', downward)]
  transfers between devices with their start and end apart: 18 -> 13, of which waited for: 12 -> 9; matrix products, arithmetic and copies ran while one was open for 3% -> 4% of each run, Pallas kernels for 26% -> 21%
where the time goes in v1:
time: 278 us; the launch traced here: 277 us
  waiting for transfers between devices  134 us (48%)
  Pallas kernels  81 us (29%)
  starting transfers between devices  29.8 us (11%)
  between operations  16.4 us (6%)
  other arithmetic  10 us (4%)
  local copies, waits for them, and re-layouts  5.66 us (2%)
    all_to_all x1, waiting for transfers between devices, on_device(): lax.all_to_all(packed, 'chan', split_axis=0, concat_axis=0, tiled=True)  66.2 us
    pallas_call x2, Pallas kernels, correlate(): pl.pallas_call(functools.partial(correlate_kernel, segs), in_specs=[whole...  51.8 us
    all_to_all x2, waiting for transfers between devices, finished(): lax.all_to_all(lag, 'seg', split_axis=0, concat_axis=0, tiled=True)  23.9 us
    ppermute x3, waiting for transfers between devices, on_device(): up = lax.ppermute(up, 'chan', upward)  22.5 us
    ppermute x3, waiting for transfers between devices, on_device(): down = lax.ppermute(down, 'chan', downward)  18.5 us
    pallas_call x1, Pallas kernels, transform(): pl.pallas_call(functools.partial(transform_kernel, layout), in_specs=[pl....  13 us
    ppermute x3, starting transfers between devices, on_device(): up = lax.ppermute(up, 'chan', upward)  10.1 us
    all_to_all x2, starting transfers between devices, finished(): lax.all_to_all(lag, 'seg', split_axis=0, concat_axis=0, tiled=True)  9.04 us
  transfers between devices with their start and end apart: 13, of which 9 were waited for; matrix products, arithmetic and copies ran while one was open for 4% of the time, Pallas kernels for 21%

profile of v1, /device:TPU:0, one launch (start us, length us, event | category | flops | bytes accessed | tf_op | source)
XLA Modules:
  0.0 276.7 jit_solution(13711831582512222382)
XLA Ops:
  6.5 6.2 %pack.1 = bf16[8,2,6,32,512]{4,3,2,1,0:T(8,128)(2,1)} custom-call(s32[12]{0:T(128)} %lengths_ref.1, s32[1]{0:T(128)} %bitcast.4.start_ref, bf16[12,256,512]{2,1,0:T(8,128)(2,1)} %x_ref.1), custom_call_target="tpu_custom_call" | custom-call | tf_op jit(solution)/shard_map/pack/pallas_call | solution.py:101
  12.8 6.5 %all-to-all-start.2 = ((bf16[8,384,512]{2,1,0:T(8,128)(2,1)}), bf16[8,384,512]{2,1,0:T(8,128)(2,1)}, u32[]{:S(2)}, u32[]{:S(2)}) async-start(bf16[8,384,512]{2,1,0:T(8,128)(2,1)} %bitcast.61), calls=%async_computation.2 | async-start | bytes 6291456 | tf_op jit(solution)/shard_map/all_to_all | solution.py:436
  23.9 0.8 fusion.4.select_ref
  24.7 66.2 %all-to-all-done.2.x_ref = bf16[8,384,512]{2,1,0:T(8,128)(2,1)} async-done(((bf16[8,384,512]{2,1,0:T(8,128)(2,1)}), bf16[8,384,512]{2,1,0:T(8,128)(2,1)}, u32[]{:S(2)}, u32[]{:S(2)}) %all-to-all-start.2) | async-done | bytes 3145760 | tf_op jit(solution)/shard_map/all_to_all | solution.py:436
  90.9 13.0 %transform.1 = (bf16[384,2304]{1,0:T(8,128)(2,1)}, bf16[192,2304]{1,0:T(8,128)(2,1)}, bf16[192,2304]{1,0:T(8,128)(2,1)}, bf16[2,2304,128]{2,1,0:T(8,128)(2,1)}) custom-call(s32[1]{0:T(128)} %bitcast.3.core_ref, bf16[8,384,512]{2,1,0:T(8,128)(2,1)} %all-to-all-done.2.x_ref, bf16[15,512,512]{2,1,0:T(8,128)(2,1)} %constant.202.clone.table_ref, ...), custom_call_target="tpu_custom_call" | custom-call | tf_op jit(solution)/shard_map/transform/pallas_call | solution.py:180
  104.0 2.3 fusion.18
  106.3 1.3 collective-permute-start.2
  107.6 1.3 collective-permute-start.4
  109.0 11.2 %collective-permute-done.2 = bf16[2304,128]{1,0:T(8,128)(2,1)S(1)} collective-permute-done((bf16[2304,128]{1,0:T(8,128)(2,1)S(1)}, bf16[2304,128]{1,0:T(8,128)(2,1)S(1)}, u32[]{:S(2)}, u32[]{:S(2)}) %collective-permute-start.2) | collective-permute-done | bytes 589856 | tf_op jit(solution)/shard_map/ppermute | solution.py:504
  120.2 5.2 %collective-permute-start.3 = (bf16[2304,128]{1,0:T(8,128)(2,1)S(1)}, bf16[2304,128]{1,0:T(8,128)(2,1)}, u32[]{:S(2)}, u32[]{:S(2)}) collective-permute-start(bf16[2304,128]{1,0:T(8,128)(2,1)S(1)} %collective-permute-done.2), channel_id=1, source_target_pairs={{0,2},{1,3},{2,4},{3,5},{4,6},{5,7},{8,10},{9,11},{10,12},{11,13},... | collective-permute-start | bytes 1769480 | tf_op jit(solution)/shard_map/ppermute | solution.py:504
  125.4 1.3 collective-permute-start.5
  126.7 0.9 copy-done.3
  127.6 5.2 %gather_bins.1.own_ref = bf16[144,32,256]{2,1,0:T(8,128)(2,1)S(1)} custom-call(bf16[6,32,2304]{2,1,0:T(8,128)(2,1)} %bitcast.64, bf16[6,32,2304]{2,1,0:T(8,128)(2,1)} %bitcast.65), custom_call_target="tpu_custom_call" | custom-call | tf_op jit(solution)/shard_map/gather_bins/pallas_call | solution.py:243
  132.9 3.6 %collective-permute-done.3 = bf16[2304,128]{1,0:T(8,128)(2,1)} collective-permute-done((bf16[2304,128]{1,0:T(8,128)(2,1)S(1)}, bf16[2304,128]{1,0:T(8,128)(2,1)}, u32[]{:S(2)}, u32[]{:S(2)}) %collective-permute-start.3) | collective-permute-done | bytes 589856 | tf_op jit(solution)/shard_map/ppermute | solution.py:504
  136.5 5.2 %collective-permute-done.5 = bf16[2304,128]{1,0:T(8,128)(2,1)} collective-permute-done((bf16[2304,128]{1,0:T(8,128)(2,1)}, bf16[2304,128]{1,0:T(8,128)(2,1)}, u32[]{:S(2)}, u32[]{:S(2)}) %collective-permute-start.5) | collective-permute-done | bytes 589856 | tf_op jit(solution)/shard_map/ppermute | solution.py:505
  141.7 3.6 %collective-permute-start.7 = (bf16[2304,128]{1,0:T(8,128)(2,1)}, bf16[2304,128]{1,0:T(8,128)(2,1)}, u32[]{:S(2)}, u32[]{:S(2)}) collective-permute-start(bf16[2304,128]{1,0:T(8,128)(2,1)} %collective-permute-done.3), channel_id=1, source_target_pairs={{0,2},{1,3},{2,4},{3,5},{4,6},{5,7},{8,10},{9,11},{10,12},{11,13},... | collective-permute-start | bytes 1769480 | tf_op jit(solution)/shard_map/ppermute | solution.py:504
  145.3 1.5 collective-permute-start.8
  146.8 1.3 add_bitcast_fusion.1
  148.1 7.7 %collective-permute-done.7 = bf16[2304,128]{1,0:T(8,128)(2,1)} collective-permute-done((bf16[2304,128]{1,0:T(8,128)(2,1)}, bf16[2304,128]{1,0:T(8,128)(2,1)}, u32[]{:S(2)}, u32[]{:S(2)}) %collective-permute-start.7) | collective-permute-done | bytes 589856 | tf_op jit(solution)/shard_map/ppermute | solution.py:504
  155.8 1.4 add_bitcast_fusion.2
  157.2 13.3 %collective-permute-done.8 = bf16[2304,128]{1,0:T(8,128)(2,1)} collective-permute-done((bf16[2304,128]{1,0:T(8,128)(2,1)}, bf16[2304,128]{1,0:T(8,128)(2,1)}, u32[]{:S(2)}, u32[]{:S(2)}) %collective-permute-start.8) | collective-permute-done | bytes 589856 | tf_op jit(solution)/shard_map/ppermute | solution.py:505
  170.5 1.1 add_bitcast_fusion
  171.7 1.8 pad_maximum_fusion.mine_ref
  174.1 0.8 and_convert_fusion.1
  174.9 1.3 slice_bitcast_fusion.4
  176.2 2.1 collective-permute-done.9.theirs_ref
  178.3 25.9 %correlate.12 = bf16[4,512,512]{2,1,0:T(8,128)(2,1)} custom-call(bf16[144,32,256]{2,1,0:T(8,128)(2,1)S(1)} %gather_bins.1.own_ref, bf16[4,2304,128]{2,1,0:T(8,128)(2,1)} %pad_maximum_fusion.mine_ref, bf16[4,2304,128]{2,1,0:T(8,128)(2,1)} %collective-permute-done.9.theirs_ref, bf16[512,768]{1,0:T(8,128)(2,1)} %get-tuple-element.427.place_ref, ...), custom_call_target="tpu_custom_call" | custom-call | tf_op jit(solution)/shard_map/correlate/pallas_call | solution.py:338
  204.3 4.5 %all-to-all-start.3 = ((bf16[4,512,512]{2,1,0:T(8,128)(2,1)}), bf16[4,512,512]{2,1,0:T(8,128)(2,1)}, u32[]{:S(2)}, u32[]{:S(2)}) async-start(bf16[4,512,512]{2,1,0:T(8,128)(2,1)} %correlate.12), calls=%async_computation.3 | async-start | bytes 4194304 | tf_op jit(solution)/shard_map/all_to_all | solution.py:522
  209.1 25.9 %correlate.13 = bf16[4,512,512]{2,1,0:T(8,128)(2,1)} custom-call(bf16[144,32,256]{2,1,0:T(8,128)(2,1)S(1)} %gather_bins.1.own_ref, bf16[4,2304,128]{2,1,0:T(8,128)(2,1)} %bitcast.63, bf16[4,2304,128]{2,1,0:T(8,128)(2,1)} %collective-permute-done.10.theirs_ref, bf16[512,768]{1,0:T(8,128)(2,1)} %get-tuple-element.426.place_ref, ...), custom_call_target="tpu_custom_call" | custom-call | tf_op jit(solution)/shard_map/correlate/pallas_call | solution.py:338
  235.0 4.6 %all-to-all-start.4 = ((bf16[4,512,512]{2,1,0:T(8,128)(2,1)}), bf16[4,512,512]{2,1,0:T(8,128)(2,1)}, u32[]{:S(2)}, u32[]{:S(2)}) async-start(bf16[4,512,512]{2,1,0:T(8,128)(2,1)} %correlate.13), calls=%async_computation.4 | async-start | bytes 4194304 | tf_op jit(solution)/shard_map/all_to_all | solution.py:522
  241.2 23.9 %all-to-all-done.4.refs_1_ = bf16[4,512,512]{2,1,0:T(8,128)(2,1)} async-done(((bf16[4,512,512]{2,1,0:T(8,128)(2,1)}), bf16[4,512,512]{2,1,0:T(8,128)(2,1)}, u32[]{:S(2)}, u32[]{:S(2)}) %all-to-all-start.4) | async-done | bytes 2097184 | tf_op jit(solution)/shard_map/all_to_all | solution.py:522
  265.1 4.7 %finish.6 = f32[32,32,512]{2,1,0:T(8,128)} custom-call(bf16[64,256]{1,0:T(8,128)(2,1)} %and_convert_fusion.2.place_ref, bf16[4,512,512]{2,1,0:T(8,128)(2,1)} %all-to-all-done.3.refs_0_, bf16[4,512,512]{2,1,0:T(8,128)(2,1)} %all-to-all-done.4.refs_1_), custom_call_target="tpu_custom_call" | custom-call | tf_op jit(solution)/shard_map/finish/pallas_call | solution.py:370
  (88 shorter events, 4.7 us)
Async XLA Ops:
  12.8 6.6 %copy-start.21 = (s32[128]{0:T(128)S(1)}, s32[128]{0:T(128)}, u32[]{:S(2)}) copy-start(s32[128]{0:T(128)} %param.31) | copy-start | bytes 1540
  12.8 6.8 %copy-start.12 = (s32[8,128]{1,0:T(8,128)S(1)}, s32[8,128]{1,0:T(8,128)}, u32[]{:S(2)}) copy-start(s32[8,128]{1,0:T(8,128)} %constant.192.clone) | copy-start | bytes 12292
  12.8 8.9 %copy-start.7 = (pred[128,384]{1,0:T(32,128)(4,1)S(1)}, pred[128,384]{1,0:T(32,128)(4,1)}, u32[]{:S(2)}) copy-start(pred[128,384]{1,0:T(32,128)(4,1)} %constant.213) | copy-start | bytes 147460
  12.8 10.5 %copy-start.20 = (s32[128]{0:T(128)S(1)}, s32[128]{0:T(128)}, u32[]{:S(2)}) copy-start(s32[128]{0:T(128)} %constant.211) | copy-start | bytes 1540
  12.8 11.1 %copy-start.6 = (s32[384]{0:T(512)S(1)}, s32[384]{0:T(512)}, u32[]{:S(2)}) copy-start(s32[384]{0:T(512)} %constant.212) | copy-start | bytes 4612
  12.8 78.1 %all-to-all-start.2 = ((bf16[8,384,512]{2,1,0:T(8,128)(2,1)}), bf16[8,384,512]{2,1,0:T(8,128)(2,1)}, u32[]{:S(2)}, u32[]{:S(2)}) async-start(bf16[8,384,512]{2,1,0:T(8,128)(2,1)} %bitcast.61), calls=%async_computation.2 | async-start | bytes 6291456 | tf_op jit(solution)/shard_map/all_to_all | solution.py:436
  19.3 184.9 %all-gather.3.cloned.1.call-start = ((), (), s32[]{:S(2)}) async-start(), calls=%async_computation.5 | async-start | bytes 2949120 | tf_op jit(solution)/shard_map/all_gather | solution.py:509
  19.4 84.6 %copy-start.10 = (pred[128]{0:T(512)(128)(4,1)}, pred[128]{0:T(512)(128)(4,1)S(1)}, u32[]{:S(2)}) copy-start(pred[128]{0:T(512)(128)(4,1)S(1)} %get-tuple-element.424) | copy-start | bytes 388
  23.2 80.7 %copy-start.15 = (s32[128]{0:T(128)}, s32[128]{0:T(128)S(1)}, u32[]{:S(2)}) copy-start(s32[128]{0:T(128)S(1)} %fusion.16) | copy-start | bytes 1540
  104.0 5.0 %copy-start.23 = (bf16[192,2304]{1,0:T(8,128)(2,1)S(1)}, bf16[192,2304]{1,0:T(8,128)(2,1)}, u32[]{:S(2)}) copy-start(bf16[192,2304]{1,0:T(8,128)(2,1)} %get-tuple-element.293) | copy-start | bytes 2654212
  106.3 13.9 %collective-permute-start.2 = (bf16[2304,128]{1,0:T(8,128)(2,1)S(1)}, bf16[2304,128]{1,0:T(8,128)(2,1)S(1)}, u32[]{:S(2)}, u32[]{:S(2)}) collective-permute-start(bf16[2304,128]{1,0:T(8,128)(2,1)S(1)} %get-tuple-element.429), channel_id=1, source_target_pairs={{0,2},{1,3},{2,4},{3,5},{4,6},{5,7},{8,10},{9,11},{10,12},{11,13},... | collective-permute-start | bytes 1769480 | tf_op jit(solution)/shard_map/ppermute | solution.py:504
  107.6 17.8 %collective-permute-start.4 = (bf16[2304,128]{1,0:T(8,128)(2,1)S(1)}, bf16[2304,128]{1,0:T(8,128)(2,1)}, u32[]{:S(2)}, u32[]{:S(2)}) collective-permute-start(bf16[2304,128]{1,0:T(8,128)(2,1)S(1)} %get-tuple-element.429), channel_id=1, source_target_pairs={{2,0},{3,1},{4,2},{5,3},{6,4},{7,5},{10,8},{11,9},{12,10},{13,11},... | collective-permute-start | bytes 1769480 | tf_op jit(solution)/shard_map/ppermute | solution.py:505
  108.9 17.8 %collective-permute-start.6 = (bf16[192,2304]{1,0:T(8,128)(2,1)S(1)}, bf16[192,2304]{1,0:T(8,128)(2,1)S(1)}, u32[]{:S(2)}, u32[]{:S(2)}) collective-permute-start(bf16[192,2304]{1,0:T(8,128)(2,1)S(1)} %copy-done.23), channel_id=1, source_target_pairs={{0,1},{1,0},{2,3},{3,2},{4,5},{5,4},{6,7},{7,6},{8,9},{9,8},{10,11... | collective-permute-start | bytes 2654216 | tf_op jit(solution)/shard_map/ppermute | solution.py:497
  120.2 16.3 %collective-permute-start.3 = (bf16[2304,128]{1,0:T(8,128)(2,1)S(1)}, bf16[2304,128]{1,0:T(8,128)(2,1)}, u32[]{:S(2)}, u32[]{:S(2)}) collective-permute-start(bf16[2304,128]{1,0:T(8,128)(2,1)S(1)} %collective-permute-done.2), channel_id=1, source_target_pairs={{0,2},{1,3},{2,4},{3,5},{4,6},{5,7},{8,10},{9,11},{10,12},{11,13},... | collective-permute-start | bytes 1769480 | tf_op jit(solution)/shard_map/ppermute | solution.py:504
  125.4 16.3 %collective-permute-start.5 = (bf16[2304,128]{1,0:T(8,128)(2,1)}, bf16[2304,128]{1,0:T(8,128)(2,1)}, u32[]{:S(2)}, u32[]{:S(2)}) collective-permute-start(bf16[2304,128]{1,0:T(8,128)(2,1)} %collective-permute-done.4), channel_id=1, source_target_pairs={{2,0},{3,1},{4,2},{5,3},{6,4},{7,5},{10,8},{11,9},{12,10},{13,11},... | collective-permute-start | bytes 1769480 | tf_op jit(solution)/shard_map/ppermute | solution.py:505
  141.7 14.0 %collective-permute-start.7 = (bf16[2304,128]{1,0:T(8,128)(2,1)}, bf16[2304,128]{1,0:T(8,128)(2,1)}, u32[]{:S(2)}, u32[]{:S(2)}) collective-permute-start(bf16[2304,128]{1,0:T(8,128)(2,1)} %collective-permute-done.3), channel_id=1, source_target_pairs={{0,2},{1,3},{2,4},{3,5},{4,6},{5,7},{8,10},{9,11},{10,12},{11,13},... | collective-permute-start | bytes 1769480 | tf_op jit(solution)/shard_map/ppermute | solution.py:504
  145.3 25.2 %collective-permute-start.8 = (bf16[2304,128]{1,0:T(8,128)(2,1)}, bf16[2304,128]{1,0:T(8,128)(2,1)}, u32[]{:S(2)}, u32[]{:S(2)}) collective-permute-start(bf16[2304,128]{1,0:T(8,128)(2,1)} %collective-permute-done.5), channel_id=1, source_target_pairs={{2,0},{3,1},{4,2},{5,3},{6,4},{7,5},{10,8},{11,9},{12,10},{13,11},... | collective-permute-start | bytes 1769480 | tf_op jit(solution)/shard_map/ppermute | solution.py:505
  171.6 1.9 copy-start.11
  171.6 1.9 copy-start.14
  171.6 2.3 copy-start.5
  171.6 2.4 copy-start.17
  171.6 2.4 copy-start.18
  173.4 4.9 %collective-permute-start.9 = (bf16[4,2304,128]{2,1,0:T(8,128)(2,1)}, bf16[4,2304,128]{2,1,0:T(8,128)(2,1)}, u32[]{:S(2)}, u32[]{:S(2)}) collective-permute-start(bf16[4,2304,128]{2,1,0:T(8,128)(2,1)} %pad_maximum_fusion.mine_ref), channel_id=1, source_target_pairs={{0,1},{1,0},{2,3},{3,2},{4,5},{5,4},{6,7},{7,6},{8,9},{9,8},{10,11... | collective-permute-start | bytes 7077896 | tf_op jit(solution)/shard_map/ppermute | solution.py:515
  174.1 4.2 %copy-start.1 = (bf16[256,256]{1,0:T(8,128)(2,1)S(1)}, bf16[256,256]{1,0:T(8,128)(2,1)}, u32[]{:S(2)}) copy-start(bf16[256,256]{1,0:T(8,128)(2,1)} %constant.205.clone.order_ref) | copy-start | bytes 393220
  204.2 4.9 %collective-permute-start.10 = (bf16[4,2304,128]{2,1,0:T(8,128)(2,1)}, bf16[4,2304,128]{2,1,0:T(8,128)(2,1)}, u32[]{:S(2)}, u32[]{:S(2)}) collective-permute-start(bf16[4,2304,128]{2,1,0:T(8,128)(2,1)} %bitcast.62), channel_id=1, source_target_pairs={{0,1},{1,0},{2,3},{3,2},{4,5},{5,4},{6,7},{7,6},{8,9},{9,8},{10,11... | collective-permute-start | bytes 7077896 | tf_op jit(solution)/shard_map/ppermute | solution.py:515
  204.3 30.7 %all-to-all-start.3 = ((bf16[4,512,512]{2,1,0:T(8,128)(2,1)}), bf16[4,512,512]{2,1,0:T(8,128)(2,1)}, u32[]{:S(2)}, u32[]{:S(2)}) async-start(bf16[4,512,512]{2,1,0:T(8,128)(2,1)} %correlate.12), calls=%async_computation.3 | async-start | bytes 4194304 | tf_op jit(solution)/shard_map/all_to_all | solution.py:522
  235.0 5.5 %copy-start.4 = (pred[64,256]{1,0:T(32,128)(4,1)S(1)}, pred[64,256]{1,0:T(32,128)(4,1)}, u32[]{:S(2)}) copy-start(pred[64,256]{1,0:T(32,128)(4,1)} %constant.201.clone) | copy-start | bytes 49156
  235.0 5.5 %copy-start.8 = (s32[256]{0:T(256)S(1)}, s32[256]{0:T(256)}, u32[]{:S(2)}) copy-start(s32[256]{0:T(256)} %constant.209) | copy-start | bytes 3076
  235.0 5.5 %copy-start.9 = (s32[256]{0:T(256)S(1)}, s32[256]{0:T(256)}, u32[]{:S(2)}) copy-start(s32[256]{0:T(256)} %constant.210) | copy-start | bytes 3076
  235.0 30.1 %all-to-all-start.4 = ((bf16[4,512,512]{2,1,0:T(8,128)(2,1)}), bf16[4,512,512]{2,1,0:T(8,128)(2,1)}, u32[]{:S(2)}, u32[]{:S(2)}) async-start(bf16[4,512,512]{2,1,0:T(8,128)(2,1)} %correlate.13), calls=%async_computation.4 | async-start | bytes 4194304 | tf_op jit(solution)/shard_map/all_to_all | solution.py:522
  241.2 28.6 %copy-start = (bf16[384,768]{1,0:T(8,128)(2,1)S(1)}, bf16[384,768]{1,0:T(8,128)(2,1)}, u32[]{:S(2)}) copy-start(bf16[384,768]{1,0:T(8,128)(2,1)} %constant.208.clone..sunk.4) | copy-start | bytes 1769476
  241.2 28.6 %copy-start.2 = (pred[384,384]{1,0:T(32,128)(4,1)S(1)}, pred[384,384]{1,0:T(32,128)(4,1)}, u32[]{:S(2)}) copy-start(pred[384,384]{1,0:T(32,128)(4,1)} %constant.265) | copy-start | bytes 442372
  (4 other events, 5.2 us)
Sparse Core Ops, SparseCore 0:
  146.9 52.3 all-gather.2

commit v2 on v1

--- a/solution.py
+++ b/solution.py
@@ -25,7 +25,7 @@
 F32 = jnp.float32
 VMEM_LIMIT = 60 * 1024 * 1024
 GROUPS = ((0,), (4,), (2, 6), (1, 7), (3, 5))
-COMPONENTS = ((0, 0), (4, 0), (2, 0), (2, 1), (1, 0), (1, 1), (3, 0), (3, 1))
+COMPONENTS = {0: (0, None), 4: (1, None), 2: (2, 3), 1: (4, 5), 3: (6, 7)}
 
 
 def phases(first, second):
@@ -52,20 +52,17 @@
     for begin in range(0, NF, TILE):
         end = min(begin + TILE, NF)
         used = []
-        for index, (root, part) in enumerate(COMPONENTS):
+        for root, (real_part, imag_part) in COMPONENTS.items():
             hit = (base[begin:end] == root).astype(np.float32)
             if not hit.any():
                 continue
-            c, s, g = cos[:, begin:end], sin[:, begin:end], sign[begin:end]
-            real = c * hit if part == 0 else g * s * hit
-            imag = -s * hit if part == 0 else g * c * hit
             block = np.zeros((PART, 2 * TILE), np.float32)
-            block[:, : end - begin] = real
-            block[:, TILE : TILE + end - begin] = imag
-            used.append((index, len(blocks)))
+            block[:, : end - begin] = cos[:, begin:end] * hit
+            block[:, TILE : TILE + end - begin] = sin[:, begin:end] * hit
+            used.append((real_part, imag_part, len(blocks)))
             blocks.append(block)
         layout.append((begin, end, used))
-    return np.stack(blocks).astype(ml_dtypes.bfloat16), layout
+    return np.stack(blocks).astype(ml_dtypes.bfloat16), sign[None, :], layout
 
 
 @functools.lru_cache(maxsize=None)
@@ -73,7 +70,7 @@
     order = bin_order()
     nearby = np.abs(order[:, None] - order[None, :]) <= SMOOTH
     counts = nearby.sum(axis=0).astype(np.float32)
-    return nearby.astype(ml_dtypes.bfloat16), (1.0 / counts)[None, :].astype(np.float32)
+    return order.astype(np.float32), (1.0 / counts)[None, :].astype(np.float32)
 
 
 @functools.lru_cache(maxsize=None)
@@ -84,14 +81,16 @@
 
 
 def pack_kernel(lengths_ref, start_ref, x_ref, out_ref):
-    core = lax.rem(pl.program_id(0), 2)
     windows, channels, samples = x_ref.shape
+    windows = windows // 2
     half = channels // 2
-    sample = start_ref[0] + lax.broadcasted_iota(jnp.int32, (half, samples), 1)
-    for w in range(windows):
+    sample = start_ref[0] + lax.broadcasted_iota(jnp.int32, (16, samples), 1)
+    for core, w in itertools.product(range(2), range(windows)):
         inside = (sample < lengths_ref[core * windows + w]).astype(F32).astype(BF16)
+        inside = jnp.concatenate([inside] * (half // 16), axis=0)
         for h in range(2):
-            out_ref[0, h, w] = x_ref[w, h * half : (h + 1) * half, :] * inside
+            rows = slice(h * half, (h + 1) * half)
+            out_ref[core, h, w] = x_ref[core * windows + w, rows, :] * inside
 
 
 def pack(strain, lengths, start, chips):
@@ -100,14 +99,14 @@
     chip_channels = channels // chips
     return pl.pallas_call(
         pack_kernel,
-        grid=(2 * chips,),
+        grid=(chips,),
         in_specs=[
             pl.BlockSpec(memory_space=pltpu.SMEM),
             pl.BlockSpec(memory_space=pltpu.SMEM),
-            pl.BlockSpec((per_core, chip_channels, samples), lambda i: (i % 2, i // 2, 0)),
+            pl.BlockSpec((windows, chip_channels, samples), lambda i: (0, i, 0)),
         ],
         out_specs=pl.BlockSpec(
-            (1, 2, per_core, chip_channels // 2, samples), lambda i: (i, 0, 0, 0, 0)
+            (2, 2, per_core, chip_channels // 2, samples), lambda i: (i, 0, 0, 0, 0)
         ),
         out_shape=jax.ShapeDtypeStruct(
             (2 * chips, 2, per_core, chip_channels // 2, samples), BF16
@@ -117,8 +116,18 @@
     )(lengths, start, strain)
 
 
-def transform_kernel(layout, core_ref, x_ref, table_ref, nearby_ref, inverse_ref, select_ref,
-                     white_ref, own_ref, other_ref, send_ref, parts, real, imag):
+def transform_kernel(layout, core_ref, x_ref, table_hbm, sign_ref, bin_row_ref, bin_column_ref,
+                     inverse_ref, select_ref,
+                     own_ref, other_ref, *rest):
+    send_refs = rest[:CLASSES]
+    parts, real, imag, white_ref, table_ref, nearby_ref, sems = rest[CLASSES:]
+    tiles = [(used[0][2], used[-1][2] + 1) for _, _, used in layout]
+    copies = [
+        pltpu.make_async_copy(table_hbm.at[a:b], table_ref.at[a:b], sems.at[i])
+        for i, (a, b) in enumerate(tiles)
+    ]
+    for copy in copies:
+        copy.start()
     slabs, rows, samples = x_ref.shape
     merge = PART // samples
     root = math.sqrt(0.5)
@@ -143,14 +152,28 @@
             parts[index, at, :] = value.astype(BF16)
         return carry
 
+    for begin in range(0, NF, 128):
+        gap = jnp.abs(bin_column_ref[begin : begin + 128, :] - bin_row_ref[...])
+        nearby_ref[begin : begin + 128, :] = jnp.where(gap <= SMOOTH, 1.0, 0.0).astype(BF16)
     lax.fori_loop(0, rows // step, fold, 0)
-    for begin, end, used in layout:
-        total = None
-        for component, block in used:
-            term = jnp.dot(parts[component], table_ref[block], preferred_element_type=F32)
-            total = term if total is None else total + term
-        real[:, begin:end] = total[:, : end - begin]
-        imag[:, begin:end] = total[:, TILE : TILE + end - begin]
+    for copy, (begin, end, used) in zip(copies, layout):
+        copy.wait()
+        straight = crossed = None
+        for real_part, imag_part, block in used:
+            term = jnp.dot(parts[real_part], table_ref[block], preferred_element_type=F32)
+            straight = term if straight is None else straight + term
+            if imag_part is None:
+                continue
+            term = jnp.dot(parts[imag_part], table_ref[block], preferred_element_type=F32)
+            crossed = term if crossed is None else crossed + term
+        width = end - begin
+        re, im = straight[:, :width], -straight[:, TILE : TILE + width]
+        if crossed is not None:
+            side = sign_ref[:, begin:end]
+            re = re + crossed[:, TILE : TILE + width] * side
+            im = im + crossed[:, :width] * side
+        real[:, begin:end] = re
+        imag[:, begin:end] = im
     re, im = real[...], imag[...]
     magnitude = jnp.sqrt(re * re + im * im).astype(BF16)
     smooth = jnp.dot(magnitude, nearby_ref[...], preferred_element_type=F32)
@@ -161,40 +184,45 @@
     core = core_ref[0]
     own_ref[...] = white_ref[pl.ds(pl.multiple_of(core * half, half), half), :]
     other_ref[...] = white_ref[pl.ds(pl.multiple_of((1 - core) * half, half), half), :]
-    lanes = send_ref.shape[2]
-    for q in range(send_ref.shape[0]):
+    lanes = send_refs[0].shape[1]
+    for q, send_ref in enumerate(send_refs):
         chosen = jnp.dot(
             select_ref[q * lanes : (q + 1) * lanes, :], white_ref[...], preferred_element_type=F32
         )
         for begin in range(0, 2 * NF, 128):
-            send_ref[q, begin : begin + 128, :] = jnp.transpose(
+            send_ref[begin : begin + 128, :] = jnp.transpose(
                 chosen[:, begin : begin + 128]
             ).astype(BF16)
 
 
 def transform(received, select, core, lanes):
     slabs, rows, samples = received.shape
-    table, layout = forward_blocks()
-    nearby, inverse = band_tables()
+    table, sign, layout = forward_blocks()
+    bins, inverse = band_tables()
     whole = pl.BlockSpec(memory_space=pltpu.VMEM)
     return pl.pallas_call(
         functools.partial(transform_kernel, layout),
-        in_specs=[pl.BlockSpec(memory_space=pltpu.SMEM)] + [whole] * 5,
-        out_specs=[whole] * 4,
+        in_specs=[pl.BlockSpec(memory_space=pltpu.SMEM), whole]
+        + [pl.BlockSpec(memory_space=pl.ANY)]
+        + [whole] * 5,
+        out_specs=[whole] * (2 + CLASSES),
         out_shape=[
-            jax.ShapeDtypeStruct((rows, 2 * NF), BF16),
             jax.ShapeDtypeStruct((rows // 2, 2 * NF), BF16),
             jax.ShapeDtypeStruct((rows // 2, 2 * NF), BF16),
-            jax.ShapeDtypeStruct((CLASSES, 2 * NF, lanes), BF16),
-        ],
+        ]
+        + [jax.ShapeDtypeStruct((2 * NF, lanes), BF16)] * CLASSES,
         scratch_shapes=[
-            pltpu.VMEM((len(COMPONENTS), rows, PART), BF16),
+            pltpu.VMEM((RADIX, rows, PART), BF16),
             pltpu.VMEM((rows, NF), F32),
             pltpu.VMEM((rows, NF), F32),
+            pltpu.VMEM((rows, 2 * NF), BF16),
+            pltpu.VMEM(table.shape, BF16),
+            pltpu.VMEM((NF, NF), BF16),
+            pltpu.SemaphoreType.DMA((len(layout),)),
         ],
         compiler_params=pltpu.CompilerParams(vmem_limit_bytes=VMEM_LIMIT),
         name="transform",
-    )(core, received, table, nearby, inverse, select)
+    )(core, received, table, sign, bins[None, :], bins[:, None], inverse, select)
 
 
 def gather_bins_kernel(mine_ref, theirs_ref, out_ref):
@@ -250,8 +278,21 @@
     )(mine, theirs)
 
 
-def correlate_kernel(segs, own_ref, mine_ref, theirs_ref, place_ref, order_ref, table_ref,
-                     out_ref, src, cross):
+def correlate_kernel(segs, mine_hbm, theirs_hbm, own_hbm, table_hbm, place_ref, order_ref,
+                     out_ref, src, cross, mine_ref, theirs_ref, own_ref, table_ref, sems):
+    copies = [
+        pltpu.make_async_copy(a, b, sems.at[i])
+        for i, (a, b) in enumerate(
+            (
+                (mine_hbm, mine_ref),
+                (theirs_hbm, theirs_ref),
+                (own_hbm, own_ref),
+                (table_hbm, table_ref),
+            )
+        )
+    ]
+    for copy in copies:
+        copy.start()
     channels = own_ref.shape[1]
     windows = place_ref.shape[1] // 128
     sources = 64
@@ -268,6 +309,7 @@
                 src[(2 + part) * windows + w + e] = jnp.where(low, i, r)
 
     for part, ref in enumerate((mine_ref, theirs_ref)):
+        copies[part].wait()
         joined = jnp.concatenate([ref[d] for d in range(ref.shape[0])], axis=1)
         spread(part, joined, place_ref)
 
@@ -308,12 +350,21 @@
             cross[c // 4, at_im, lanes] = im.astype(BF16)
         return carry
 
-    lax.fori_loop(0, NF // 16, bins, 0, unroll=4)
+    copies[2].wait()
+    lax.fori_loop(0, NF // 16, bins, 0, unroll=8)
 
     rows = TILE // segs
 
     def lags(i, carry):
-        lag = jnp.dot(table_ref[...], cross[i], preferred_element_type=F32).astype(BF16)
+        lag = jnp.concatenate(
+            [
+                jnp.dot(
+                    table_ref[n : n + TILE, :], cross[i], preferred_element_type=F32
+                ).astype(BF16)
+                for n in range(0, LAGS, TILE)
+            ],
+            axis=0,
+        )
         turned = lax.dot_general(
             order_ref[...], lag, (((1,), (1,)), ((), ())), preferred_element_type=F32
         ).astype(BF16)
@@ -322,6 +373,7 @@
             out_ref[g, at, :] = turned[g * rows : (g + 1) * rows, :]
         return carry
 
+    copies[3].wait()
     lax.fori_loop(0, channels // 4, lags, 0)
 
 
@@ -337,16 +389,21 @@
     whole = pl.BlockSpec(memory_space=pltpu.VMEM)
     return pl.pallas_call(
         functools.partial(correlate_kernel, segs),
-        in_specs=[whole] * 6,
+        in_specs=[pl.BlockSpec(memory_space=pl.ANY)] * 4 + [whole] * 2,
         out_specs=whole,
         out_shape=jax.ShapeDtypeStruct((segs, channels * group, LAGS), BF16),
         scratch_shapes=[
             pltpu.VMEM((4 * windows, NF, 128), F32),
             pltpu.VMEM((channels // 4, 2 * NF, TILE), BF16),
+            pltpu.VMEM(mine.shape, BF16),
+            pltpu.VMEM(theirs.shape, BF16),
+            pltpu.VMEM(own.shape, BF16),
+            pltpu.VMEM(table.shape, BF16),
+            pltpu.SemaphoreType.DMA((4,)),
         ],
         compiler_params=pltpu.CompilerParams(vmem_limit_bytes=VMEM_LIMIT),
         name="correlate",
-    )(own, mine, theirs, place, order, table)
+    )(mine, theirs, own, table, place, order)
 
 
 def finish_kernel(scale, place_ref, *refs):
@@ -365,7 +422,7 @@
 
 def finish(parts, place, scale, block, channels):
     segs, rows, _ = parts[0].shape
-    step = 8
+    step = math.gcd(channels, 16)
     piece = pl.BlockSpec((segs, rows * step // channels, LAGS), lambda i: (0, i, 0))
     return pl.pallas_call(
         functools.partial(finish_kernel, scale),
@@ -493,7 +550,7 @@
         & (row_pair[:, None] == (column // group % 2)[None, :])
     ).astype(BF16)
 
-    white, own, other, sends = transform(received, select, my_core, lanes)
+    own, other, *sends = transform(received, select, my_core, lanes)
     own_other = lax.ppermute(other, "chan", core_swap)
     shape = (per_core, channels, 2 * NF)
     bins = gather_bins(own.reshape(shape), own_other.reshape(shape))
@@ -528,8 +585,8 @@
     second_lag = stacks(second, placing[1])
     seated = finished([first_lag, second_lag])
 
-    def add_unseated(total):
-        out = slot >= cap
+    def add_unseated(turn, total):
+        out = (slot >= cap) & (turn < full)
         at = jnp.sum(jnp.where(at_spot & here & out, local[None, None, :] + 1, 0), axis=-1) - 1
         wanted = (
             (jnp.tile(at, (1, per_core))[:, :, None] == row_channel[None, None, :])
@@ -539,6 +596,8 @@
         for w in range(per_core):
             spot[w, :, w] = np.eye(spots)[:, None, :]
         spot = jnp.asarray(spot.reshape(per_core * spots, -1), BF16)
+        first = my_core[0] == 0
+        white = jnp.concatenate([jnp.where(first, own, other), jnp.where(first, other, own)])
         lags = []
         for q in range(CLASSES):
             mine = jnp.einsum("sr,rk->ks", wanted[q], white, preferred_element_type=F32)
@@ -548,7 +607,7 @@
 
     _, stacked = lax.while_loop(
         lambda carry: carry[0] < full,
-        lambda carry: (carry[0] + 1, add_unseated(carry[1])),
+        lambda carry: (carry[0] + 1, add_unseated(*carry)),
         (jnp.zeros((), jnp.int32), seated),
     )
     return stacked

time: 278 us -> 265 us (0.953)
  Pallas kernels: 81 us -> 70 us
    pallas_call x3, Pallas kernels: 58 us -> 50.1 us  [the longest x2 45.9 us: correlate(): pl.pallas_call(functools.partial(correlate_kernel, segs), in_specs=[pl.Bl...]
    ppermute x3, waiting for transfers between devices: 18.5 us -> 13 us  [on_device(): down = lax.ppermute(down, 'chan', downward)]
    all_gather x1, waiting for transfers between devices: 0.01 us -> 3.52 us  [on_device(): second = lax.all_gather(second, 'chan', axis_index_groups=lines)]
  transfers between devices with their start and end apart: 13 -> 13, of which waited for: 9 -> 11; matrix products, arithmetic and copies ran while one was open for 4% -> 5% of each run, Pallas kernels for 21% -> 19%
where the time goes in v2:
time: 265 us; the launch traced here: 264 us
  waiting for transfers between devices  134 us (51%)
  Pallas kernels  70 us (26%)
  starting transfers between devices  29.6 us (11%)
  between operations  16.6 us (6%)
  other arithmetic  10.3 us (4%)
  local copies, waits for them, and re-layouts  3.64 us (1%)
    all_to_all x1, waiting for transfers between devices, on_device(): lax.all_to_all(packed, 'chan', split_axis=0, concat_axis=0, tiled=True)  66 us
    pallas_call x2, Pallas kernels, correlate(): pl.pallas_call(functools.partial(correlate_kernel, segs), in_specs=[pl.Bl...  45.9 us
    all_to_all x2, waiting for transfers between devices, finished(): lax.all_to_all(lag, 'seg', split_axis=0, concat_axis=0, tiled=True)  25.1 us
    ppermute x3, waiting for transfers between devices, on_device(): up = lax.ppermute(up, 'chan', upward)  23.4 us
    ppermute x3, waiting for transfers between devices, on_device(): down = lax.ppermute(down, 'chan', downward)  13 us
    pallas_call x1, Pallas kernels, transform(): pl.pallas_call(functools.partial(transform_kernel, layout), in_specs=[pl....  11.3 us
    ppermute x3, starting transfers between devices, on_device(): up = lax.ppermute(up, 'chan', upward)  10 us
    all_to_all x2, starting transfers between devices, finished(): lax.all_to_all(lag, 'seg', split_axis=0, concat_axis=0, tiled=True)  8.91 us
  transfers between devices with their start and end apart: 13, of which 11 were waited for; matrix products, arithmetic and copies ran while one was open for 5% of the time, Pallas kernels for 19%

profile of v2, /device:TPU:0, one launch (start us, length us, event | category | flops | bytes accessed | tf_op | source)
XLA Modules:
  0.0 264.0 jit_solution(18209717269406862430)
XLA Ops:
  6.5 4.2 %pack.1 = bf16[8,2,6,32,512]{4,3,2,1,0:T(8,128)(2,1)} custom-call(s32[12]{0:T(128)} %lengths_ref.1, s32[1]{0:T(128)} %bitcast.4.start_ref, bf16[12,256,512]{2,1,0:T(8,128)(2,1)} %x_ref.1), custom_call_target="tpu_custom_call" | custom-call | tf_op jit(solution)/shard_map/pack/pallas_call | solution.py:100
  10.8 6.5 %all-to-all-start.2 = ((bf16[8,384,512]{2,1,0:T(8,128)(2,1)}), bf16[8,384,512]{2,1,0:T(8,128)(2,1)}, u32[]{:S(2)}, u32[]{:S(2)}) async-start(bf16[8,384,512]{2,1,0:T(8,128)(2,1)} %bitcast.49), calls=%async_computation.2 | async-start | bytes 6291456 | tf_op jit(solution)/shard_map/all_to_all | solution.py:493
  22.1 0.8 fusion.9.select_ref
  22.9 66.0 %all-to-all-done.2.x_ref = bf16[8,384,512]{2,1,0:T(8,128)(2,1)} async-done(((bf16[8,384,512]{2,1,0:T(8,128)(2,1)}), bf16[8,384,512]{2,1,0:T(8,128)(2,1)}, u32[]{:S(2)}, u32[]{:S(2)}) %all-to-all-start.2) | async-done | bytes 3145760 | tf_op jit(solution)/shard_map/all_to_all | solution.py:493
  89.0 11.3 %transform.1 = (bf16[192,2304]{1,0:T(8,128)(2,1)S(1)}, bf16[192,2304]{1,0:T(8,128)(2,1)S(1)}, bf16[2304,128]{1,0:T(8,128)(2,1)}, bf16[2304,128]{1,0:T(8,128)(2,1)}) custom-call(s32[1]{0:T(128)} %bitcast.3.core_ref, bf16[8,384,512]{2,1,0:T(8,128)(2,1)} %all-to-all-done.2.x_ref, bf16[9,512,512]{2,1,0:T(8,128)(2,1)} %constant.205.clone.table_hbm, ...), custom_call_target="tpu_custom_call" | custom-call | tf_op jit(solution)/shard_map/transform/pallas_call | solution.py:203
  100.3 2.1 collective-permute-start.3
  102.4 1.3 collective-permute-start.2
  103.7 10.8 %collective-permute-done.3 = bf16[2304,128]{1,0:T(8,128)(2,1)} collective-permute-done((bf16[2304,128]{1,0:T(8,128)(2,1)}, bf16[2304,128]{1,0:T(8,128)(2,1)}, u32[]{:S(2)}, u32[]{:S(2)}) %collective-permute-start.3) | collective-permute-done | bytes 589856 | tf_op jit(solution)/shard_map/ppermute | solution.py:561
  114.5 5.2 %collective-permute-start.4 = (bf16[2304,128]{1,0:T(8,128)(2,1)}, bf16[2304,128]{1,0:T(8,128)(2,1)}, u32[]{:S(2)}, u32[]{:S(2)}) collective-permute-start(bf16[2304,128]{1,0:T(8,128)(2,1)} %collective-permute-done.3), channel_id=1, source_target_pairs={{0,2},{1,3},{2,4},{3,5},{4,6},{5,7},{8,10},{9,11},{10,12},{11,13},... | collective-permute-start | bytes 1769480 | tf_op jit(solution)/shard_map/ppermute | solution.py:561
  119.7 1.3 collective-permute-start.5
  121.1 0.9 copy-done.5
  121.9 5.0 %gather_bins.1.own_hbm = bf16[144,32,256]{2,1,0:T(8,128)(2,1)S(1)} custom-call(bf16[6,32,2304]{2,1,0:T(8,128)(2,1)S(1)} %bitcast.48, bf16[6,32,2304]{2,1,0:T(8,128)(2,1)} %bitcast.52), custom_call_target="tpu_custom_call" | custom-call | tf_op jit(solution)/shard_map/gather_bins/pallas_call | solution.py:271
  126.9 4.1 %collective-permute-done.4 = bf16[2304,128]{1,0:T(8,128)(2,1)} collective-permute-done((bf16[2304,128]{1,0:T(8,128)(2,1)}, bf16[2304,128]{1,0:T(8,128)(2,1)}, u32[]{:S(2)}, u32[]{:S(2)}) %collective-permute-start.4) | collective-permute-done | bytes 589856 | tf_op jit(solution)/shard_map/ppermute | solution.py:561
  131.0 4.9 %collective-permute-done.5 = bf16[2304,128]{1,0:T(8,128)(2,1)} collective-permute-done((bf16[2304,128]{1,0:T(8,128)(2,1)}, bf16[2304,128]{1,0:T(8,128)(2,1)}, u32[]{:S(2)}, u32[]{:S(2)}) %collective-permute-start.5) | collective-permute-done | bytes 589856 | tf_op jit(solution)/shard_map/ppermute | solution.py:562
  135.9 2.7 %collective-permute-start.7 = (bf16[2304,128]{1,0:T(8,128)(2,1)}, bf16[2304,128]{1,0:T(8,128)(2,1)S(1)}, u32[]{:S(2)}, u32[]{:S(2)}) collective-permute-start(bf16[2304,128]{1,0:T(8,128)(2,1)} %collective-permute-done.4), channel_id=1, source_target_pairs={{0,2},{1,3},{2,4},{3,5},{4,6},{5,7},{8,10},{9,11},{10,12},{11,13},... | collective-permute-start | bytes 1769480 | tf_op jit(solution)/shard_map/ppermute | solution.py:561
  138.7 1.5 collective-permute-start.8
  140.2 1.3 add_bitcast_fusion.1
  141.5 8.5 %collective-permute-done.7 = bf16[2304,128]{1,0:T(8,128)(2,1)S(1)} collective-permute-done((bf16[2304,128]{1,0:T(8,128)(2,1)}, bf16[2304,128]{1,0:T(8,128)(2,1)S(1)}, u32[]{:S(2)}, u32[]{:S(2)}) %collective-permute-start.7) | collective-permute-done | bytes 589856 | tf_op jit(solution)/shard_map/ppermute | solution.py:561
  150.0 1.2 add_bitcast_fusion.2
  151.2 8.1 %collective-permute-done.8 = bf16[2304,128]{1,0:T(8,128)(2,1)S(1)} collective-permute-done((bf16[2304,128]{1,0:T(8,128)(2,1)}, bf16[2304,128]{1,0:T(8,128)(2,1)S(1)}, u32[]{:S(2)}, u32[]{:S(2)}) %collective-permute-start.8) | collective-permute-done | bytes 589856 | tf_op jit(solution)/shard_map/ppermute | solution.py:562
  159.3 1.1 add_bitcast_fusion
  160.5 1.7 pad_maximum_fusion.3.mine_hbm
  163.6 1.3 slice_bitcast_fusion.4
  164.9 2.2 collective-permute-done.9.theirs_hbm
  167.1 22.9 %correlate.10 = bf16[4,512,512]{2,1,0:T(8,128)(2,1)} custom-call(bf16[4,2304,128]{2,1,0:T(8,128)(2,1)} %pad_maximum_fusion.3.mine_hbm, bf16[4,2304,128]{2,1,0:T(8,128)(2,1)} %collective-permute-done.9.theirs_hbm, bf16[144,32,256]{2,1,0:T(8,128)(2,1)S(1)} %gather_bins.1.own_hbm, bf16[512,2304]{1,0:T(8,128)(2,1)} %constant.210.clone.table_hbm, ...), custom_call_target="tpu_custom_call" | custom-call | tf_op jit(solution)/shard_map/correlate/pallas_call | solution.py:390
  190.0 3.5 %all-gather.3.cloned.1.call-done = bf16[9216,128]{1,0:T(8,128)(2,1)} async-done(((bf16[2304,128]{1,0:T(8,128)(2,1)}), bf16[9216,128]{1,0:T(8,128)(2,1)}) %all-gather.3.cloned.1.call-update) | async-done | bytes 2359312 | tf_op jit(solution)/shard_map/all_gather | solution.py:566
  193.6 4.5 %all-to-all-start.3 = ((bf16[4,512,512]{2,1,0:T(8,128)(2,1)}), bf16[4,512,512]{2,1,0:T(8,128)(2,1)}, u32[]{:S(2)}, u32[]{:S(2)}) async-start(bf16[4,512,512]{2,1,0:T(8,128)(2,1)} %correlate.10), calls=%async_computation.3 | async-start | bytes 4194304 | tf_op jit(solution)/shard_map/all_to_all | solution.py:579
  198.4 23.0 %correlate.11 = bf16[4,512,512]{2,1,0:T(8,128)(2,1)} custom-call(bf16[4,2304,128]{2,1,0:T(8,128)(2,1)} %bitcast.51, bf16[4,2304,128]{2,1,0:T(8,128)(2,1)} %collective-permute-done.10.theirs_hbm, bf16[144,32,256]{2,1,0:T(8,128)(2,1)S(1)} %gather_bins.1.own_hbm, bf16[512,2304]{1,0:T(8,128)(2,1)} %constant.210.clone.table_hbm, ...), custom_call_target="tpu_custom_call" | custom-call | tf_op jit(solution)/shard_map/correlate/pallas_call | solution.py:390
  221.5 2.5 all-to-all-done.3.refs_0_
  223.9 4.5 %all-to-all-start.4 = ((bf16[4,512,512]{2,1,0:T(8,128)(2,1)}), bf16[4,512,512]{2,1,0:T(8,128)(2,1)}, u32[]{:S(2)}, u32[]{:S(2)}) async-start(bf16[4,512,512]{2,1,0:T(8,128)(2,1)} %correlate.11), calls=%async_computation.4 | async-start | bytes 4194304 | tf_op jit(solution)/shard_map/all_to_all | solution.py:579
  230.8 22.7 %all-to-all-done.4.refs_1_ = bf16[4,512,512]{2,1,0:T(8,128)(2,1)} async-done(((bf16[4,512,512]{2,1,0:T(8,128)(2,1)}), bf16[4,512,512]{2,1,0:T(8,128)(2,1)}, u32[]{:S(2)}, u32[]{:S(2)}) %all-to-all-start.4) | async-done | bytes 2097184 | tf_op jit(solution)/shard_map/all_to_all | solution.py:579
  253.5 3.6 %finish.5 = f32[32,32,512]{2,1,0:T(8,128)} custom-call(bf16[64,256]{1,0:T(8,128)(2,1)} %and_convert_fusion.2.place_ref, bf16[4,512,512]{2,1,0:T(8,128)(2,1)} %all-to-all-done.3.refs_0_, bf16[4,512,512]{2,1,0:T(8,128)(2,1)} %all-to-all-done.4.refs_1_), custom_call_target="tpu_custom_call" | custom-call | tf_op jit(solution)/shard_map/finish/pallas_call | solution.py:427
  (100 shorter events, 6.4 us)
Async XLA Ops:
  10.8 9.0 %copy-start.11 = (pred[128,384]{1,0:T(32,128)(4,1)S(1)}, pred[128,384]{1,0:T(32,128)(4,1)}, u32[]{:S(2)}) copy-start(pred[128,384]{1,0:T(32,128)(4,1)} %constant.218) | copy-start | bytes 147460
  10.8 11.1 %copy-start.27 = (s32[128]{0:T(128)S(1)}, s32[128]{0:T(128)}, u32[]{:S(2)}) copy-start(s32[128]{0:T(128)} %constant.216) | copy-start | bytes 1540
  10.8 11.3 %copy-start.9 = (s32[384]{0:T(512)S(1)}, s32[384]{0:T(512)}, u32[]{:S(2)}) copy-start(s32[384]{0:T(512)} %constant.217) | copy-start | bytes 4612
  10.8 78.1 %all-to-all-start.2 = ((bf16[8,384,512]{2,1,0:T(8,128)(2,1)}), bf16[8,384,512]{2,1,0:T(8,128)(2,1)}, u32[]{:S(2)}, u32[]{:S(2)}) async-start(bf16[8,384,512]{2,1,0:T(8,128)(2,1)} %bitcast.49), calls=%async_computation.2 | async-start | bytes 6291456 | tf_op jit(solution)/shard_map/all_to_all | solution.py:493
  17.3 176.3 %all-gather.3.cloned.1.call-start = ((), (), s32[]{:S(2)}) async-start(), calls=%async_computation.5 | async-start | bytes 2949120 | tf_op jit(solution)/shard_map/all_gather | solution.py:566
  17.4 71.5 %copy-start.16 = (pred[128]{0:T(512)(128)(4,1)}, pred[128]{0:T(512)(128)(4,1)S(1)}, u32[]{:S(2)}) copy-start(pred[128]{0:T(512)(128)(4,1)S(1)} %get-tuple-element.556) | copy-start | bytes 388
  17.4 71.5 %copy-start.18 = (s32[128]{0:T(128)}, s32[128]{0:T(128)S(1)}, u32[]{:S(2)}) copy-start(s32[128]{0:T(128)S(1)} %get-tuple-element.435) | copy-start | bytes 1540
  17.6 71.3 %copy-start.20 = (s32[8,128]{1,0:T(8,128)}, s32[8,128]{1,0:T(8,128)S(1)}, u32[]{:S(2)}) copy-start(s32[8,128]{1,0:T(8,128)S(1)} %add_select_fusion.1) | copy-start | bytes 12292
  21.2 67.7 %copy-start.21 = (s32[128]{0:T(128)}, s32[128]{0:T(128)S(1)}, u32[]{:S(2)}) copy-start(s32[128]{0:T(128)S(1)} %get-tuple-element.557) | copy-start | bytes 1540
  21.2 67.7 %copy-start.14 = (pred[2,128]{1,0:T(4,128)(4,1)}, pred[2,128]{1,0:T(4,128)(4,1)S(1)}, u32[]{:S(2)}) copy-start(pred[2,128]{1,0:T(4,128)(4,1)S(1)} %iota_compare_fusion.5) | copy-start | bytes 772
  100.2 20.8 %copy-start.2 = (bf16[192,2304]{1,0:T(8,128)(2,1)}, bf16[192,2304]{1,0:T(8,128)(2,1)S(1)}, u32[]{:S(2)}) copy-start(bf16[192,2304]{1,0:T(8,128)(2,1)S(1)} %get-tuple-element.555) | copy-start | bytes 2654212
  100.2 20.8 %copy-start.1 = (bf16[192,2304]{1,0:T(8,128)(2,1)}, bf16[192,2304]{1,0:T(8,128)(2,1)S(1)}, u32[]{:S(2)}) copy-start(bf16[192,2304]{1,0:T(8,128)(2,1)S(1)} %get-tuple-element.554) | copy-start | bytes 2654212
  100.3 14.3 %collective-permute-start.3 = (bf16[2304,128]{1,0:T(8,128)(2,1)}, bf16[2304,128]{1,0:T(8,128)(2,1)}, u32[]{:S(2)}, u32[]{:S(2)}) collective-permute-start(bf16[2304,128]{1,0:T(8,128)(2,1)} %get-tuple-element.250), channel_id=1, source_target_pairs={{0,2},{1,3},{2,4},{3,5},{4,6},{5,7},{8,10},{9,11},{10,12},{11,13},... | collective-permute-start | bytes 1769480 | tf_op jit(solution)/shard_map/ppermute | solution.py:561
  102.4 17.4 %collective-permute-start.2 = (bf16[2304,128]{1,0:T(8,128)(2,1)}, bf16[2304,128]{1,0:T(8,128)(2,1)}, u32[]{:S(2)}, u32[]{:S(2)}) collective-permute-start(bf16[2304,128]{1,0:T(8,128)(2,1)} %get-tuple-element.250), channel_id=1, source_target_pairs={{2,0},{3,1},{4,2},{5,3},{6,4},{7,5},{10,8},{11,9},{12,10},{13,11},... | collective-permute-start | bytes 1769480 | tf_op jit(solution)/shard_map/ppermute | solution.py:562
  103.7 17.4 %collective-permute-start.6 = (bf16[192,2304]{1,0:T(8,128)(2,1)S(1)}, bf16[192,2304]{1,0:T(8,128)(2,1)S(1)}, u32[]{:S(2)}, u32[]{:S(2)}) collective-permute-start(bf16[192,2304]{1,0:T(8,128)(2,1)S(1)} %get-tuple-element.555), channel_id=1, source_target_pairs={{0,1},{1,0},{2,3},{3,2},{4,5},{5,4},{6,7},{7,6},{8,9},{9,8},{10,11... | collective-permute-start | bytes 2654216 | tf_op jit(solution)/shard_map/ppermute | solution.py:554
  114.5 16.5 %collective-permute-start.4 = (bf16[2304,128]{1,0:T(8,128)(2,1)}, bf16[2304,128]{1,0:T(8,128)(2,1)}, u32[]{:S(2)}, u32[]{:S(2)}) collective-permute-start(bf16[2304,128]{1,0:T(8,128)(2,1)} %collective-permute-done.3), channel_id=1, source_target_pairs={{0,2},{1,3},{2,4},{3,5},{4,6},{5,7},{8,10},{9,11},{10,12},{11,13},... | collective-permute-start | bytes 1769480 | tf_op jit(solution)/shard_map/ppermute | solution.py:561
  119.7 16.2 %collective-permute-start.5 = (bf16[2304,128]{1,0:T(8,128)(2,1)}, bf16[2304,128]{1,0:T(8,128)(2,1)}, u32[]{:S(2)}, u32[]{:S(2)}) collective-permute-start(bf16[2304,128]{1,0:T(8,128)(2,1)} %collective-permute-done.2), channel_id=1, source_target_pairs={{2,0},{3,1},{4,2},{5,3},{6,4},{7,5},{10,8},{11,9},{12,10},{13,11},... | collective-permute-start | bytes 1769480 | tf_op jit(solution)/shard_map/ppermute | solution.py:562
  135.9 14.0 %collective-permute-start.7 = (bf16[2304,128]{1,0:T(8,128)(2,1)}, bf16[2304,128]{1,0:T(8,128)(2,1)S(1)}, u32[]{:S(2)}, u32[]{:S(2)}) collective-permute-start(bf16[2304,128]{1,0:T(8,128)(2,1)} %collective-permute-done.4), channel_id=1, source_target_pairs={{0,2},{1,3},{2,4},{3,5},{4,6},{5,7},{8,10},{9,11},{10,12},{11,13},... | collective-permute-start | bytes 1769480 | tf_op jit(solution)/shard_map/ppermute | solution.py:561
  138.7 20.6 %collective-permute-start.8 = (bf16[2304,128]{1,0:T(8,128)(2,1)}, bf16[2304,128]{1,0:T(8,128)(2,1)S(1)}, u32[]{:S(2)}, u32[]{:S(2)}) collective-permute-start(bf16[2304,128]{1,0:T(8,128)(2,1)} %collective-permute-done.5), channel_id=1, source_target_pairs={{2,0},{3,1},{4,2},{5,3},{6,4},{7,5},{10,8},{11,9},{12,10},{13,11},... | collective-permute-start | bytes 1769480 | tf_op jit(solution)/shard_map/ppermute | solution.py:562
  141.5 18.9 %copy-start.6 = (bf16[2304,128]{1,0:T(8,128)(2,1)S(1)}, bf16[2304,128]{1,0:T(8,128)(2,1)}, u32[]{:S(2)}) copy-start(bf16[2304,128]{1,0:T(8,128)(2,1)} %get-tuple-element.250) | copy-start | bytes 1769476
  162.2 4.9 %collective-permute-start.9 = (bf16[4,2304,128]{2,1,0:T(8,128)(2,1)}, bf16[4,2304,128]{2,1,0:T(8,128)(2,1)}, u32[]{:S(2)}, u32[]{:S(2)}) collective-permute-start(bf16[4,2304,128]{2,1,0:T(8,128)(2,1)} %pad_maximum_fusion.3.mine_hbm), channel_id=1, source_target_pairs={{0,1},{1,0},{2,3},{3,2},{4,5},{5,4},{6,7},{7,6},{8,9},{9,8},{10,11... | collective-permute-start | bytes 7077896 | tf_op jit(solution)/shard_map/ppermute | solution.py:572
  193.6 4.9 %collective-permute-start.10 = (bf16[4,2304,128]{2,1,0:T(8,128)(2,1)}, bf16[4,2304,128]{2,1,0:T(8,128)(2,1)}, u32[]{:S(2)}, u32[]{:S(2)}) collective-permute-start(bf16[4,2304,128]{2,1,0:T(8,128)(2,1)} %bitcast.50), channel_id=1, source_target_pairs={{0,1},{1,0},{2,3},{3,2},{4,5},{5,4},{6,7},{7,6},{8,9},{9,8},{10,11... | collective-permute-start | bytes 7077896 | tf_op jit(solution)/shard_map/ppermute | solution.py:572
  193.6 30.3 %all-to-all-start.3 = ((bf16[4,512,512]{2,1,0:T(8,128)(2,1)}), bf16[4,512,512]{2,1,0:T(8,128)(2,1)}, u32[]{:S(2)}, u32[]{:S(2)}) async-start(bf16[4,512,512]{2,1,0:T(8,128)(2,1)} %correlate.10), calls=%async_computation.3 | async-start | bytes 4194304 | tf_op jit(solution)/shard_map/all_to_all | solution.py:579
  221.4 8.6 %copy-start.7 = (pred[64,256]{1,0:T(32,128)(4,1)S(1)}, pred[64,256]{1,0:T(32,128)(4,1)}, u32[]{:S(2)}) copy-start(pred[64,256]{1,0:T(32,128)(4,1)} %constant.204.clone) | copy-start | bytes 49156
  221.4 8.6 %copy-start.12 = (s32[256]{0:T(256)S(1)}, s32[256]{0:T(256)}, u32[]{:S(2)}) copy-start(s32[256]{0:T(256)} %constant.214) | copy-start | bytes 3076
  221.4 8.6 %copy-start.13 = (s32[256]{0:T(256)S(1)}, s32[256]{0:T(256)}, u32[]{:S(2)}) copy-start(s32[256]{0:T(256)} %constant.215) | copy-start | bytes 3076
  223.9 29.6 %all-to-all-start.4 = ((bf16[4,512,512]{2,1,0:T(8,128)(2,1)}), bf16[4,512,512]{2,1,0:T(8,128)(2,1)}, u32[]{:S(2)}, u32[]{:S(2)}) async-start(bf16[4,512,512]{2,1,0:T(8,128)(2,1)} %correlate.11), calls=%async_computation.4 | async-start | bytes 4194304 | tf_op jit(solution)/shard_map/all_to_all | solution.py:579
  230.8 26.3 %copy-start = (bf16[384,768]{1,0:T(8,128)(2,1)S(1)}, bf16[384,768]{1,0:T(8,128)(2,1)}, u32[]{:S(2)}) copy-start(bf16[384,768]{1,0:T(8,128)(2,1)} %constant.213.clone..sunk.4) | copy-start | bytes 1769476
  230.8 26.3 %copy-start.4 = (pred[384,384]{1,0:T(32,128)(4,1)S(1)}, pred[384,384]{1,0:T(32,128)(4,1)}, u32[]{:S(2)}) copy-start(pred[384,384]{1,0:T(32,128)(4,1)} %constant.280) | copy-start | bytes 442372
  230.8 26.3 %copy-start.10 = (s32[384]{0:T(512)S(1)}, s32[384]{0:T(512)}, u32[]{:S(2)}) copy-start(s32[384]{0:T(512)} %constant.217) | copy-start | bytes 4612
  230.8 26.4 %copy-start.17 = (pred[128]{0:T(512)(128)(4,1)S(1)}, pred[128]{0:T(512)(128)(4,1)}, u32[]{:S(2)}) copy-start(pred[128]{0:T(512)(128)(4,1)} %copy-done.16) | copy-start | bytes 388
  230.8 26.4 %copy-start.29 = (s32[128]{0:T(128)S(1)}, s32[128]{0:T(128)}, u32[]{:S(2)}) copy-start(s32[128]{0:T(128)} %get-tuple-element.558) | copy-start | bytes 1540
  (11 other events, 32.8 us)
Sparse Core Ops, SparseCore 0:
  140.3 53.2 all-gather.2

commit v3 on v2

--- a/solution.py
+++ b/solution.py
@@ -118,7 +118,7 @@
 
 def transform_kernel(layout, core_ref, x_ref, table_hbm, sign_ref, bin_row_ref, bin_column_ref,
                      inverse_ref, select_ref,
-                     own_ref, other_ref, *rest):
+                     own_hbm, other_hbm, *rest):
     send_refs = rest[:CLASSES]
     parts, real, imag, white_ref, table_ref, nearby_ref, sems = rest[CLASSES:]
     tiles = [(used[0][2], used[-1][2] + 1) for _, _, used in layout]
@@ -182,8 +182,16 @@
     white_ref[:, NF:] = (imag[...] * inverse).astype(BF16)
     half = rows // 2
     core = core_ref[0]
-    own_ref[...] = white_ref[pl.ds(pl.multiple_of(core * half, half), half), :]
-    other_ref[...] = white_ref[pl.ds(pl.multiple_of((1 - core) * half, half), half), :]
+    halves = [
+        pltpu.make_async_copy(
+            white_ref.at[pl.ds(pl.multiple_of(side * half, half), half), :],
+            ref,
+            sems.at[len(copies) + i],
+        )
+        for i, (side, ref) in enumerate(((core, own_hbm), (1 - core, other_hbm)))
+    ]
+    for copy in halves:
+        copy.start()
     lanes = send_refs[0].shape[1]
     for q, send_ref in enumerate(send_refs):
         chosen = jnp.dot(
@@ -193,6 +201,8 @@
             send_ref[begin : begin + 128, :] = jnp.transpose(
                 chosen[:, begin : begin + 128]
             ).astype(BF16)
+    for copy in halves:
+        copy.wait()
 
 
 def transform(received, select, core, lanes):
@@ -205,7 +215,7 @@
         in_specs=[pl.BlockSpec(memory_space=pltpu.SMEM), whole]
         + [pl.BlockSpec(memory_space=pl.ANY)]
         + [whole] * 5,
-        out_specs=[whole] * (2 + CLASSES),
+        out_specs=[pl.BlockSpec(memory_space=pl.ANY)] * 2 + [whole] * CLASSES,
         out_shape=[
             jax.ShapeDtypeStruct((rows // 2, 2 * NF), BF16),
             jax.ShapeDtypeStruct((rows // 2, 2 * NF), BF16),
@@ -218,7 +228,7 @@
             pltpu.VMEM((rows, 2 * NF), BF16),
             pltpu.VMEM(table.shape, BF16),
             pltpu.VMEM((NF, NF), BF16),
-            pltpu.SemaphoreType.DMA((len(layout),)),
+            pltpu.SemaphoreType.DMA((len(layout) + 2,)),
         ],
         compiler_params=pltpu.CompilerParams(vmem_limit_bytes=VMEM_LIMIT),
         name="transform",
@@ -228,6 +238,7 @@
 def gather_bins_kernel(mine_ref, theirs_ref, out_ref):
     windows, channels, _ = mine_ref.shape
     lane = lax.broadcasted_iota(jnp.int32, (channels, 128), 1)
+    odd = lax.broadcasted_iota(jnp.int32, (channels, 128), 0) % 2 == 1
     upper = [((lane // (8 << bit)) % 2) == 1 for bit in range(4)]
 
     def turned(tiles):
@@ -250,16 +261,20 @@
         return tiles
 
     def tile(i, carry):
-        values = []
-        for part in range(2):
-            at = pl.ds(pl.multiple_of(part * NF + i * 128, 128), 128)
-            for ref in (mine_ref, theirs_ref):
-                values += [ref[w, :, at].astype(F32) for w in range(windows)]
+        at = pl.ds(pl.multiple_of(i * 128, 128), 128)
+        at_im = pl.ds(pl.multiple_of(NF + i * 128, 128), 128)
+        first_half, second_half = [], []
+        for ref in (mine_ref, theirs_ref):
+            for w in range(windows):
+                re, im = ref[w, :, at].astype(F32), ref[w, :, at_im].astype(F32)
+                first_half.append(jnp.where(odd, -im, re))
+                second_half.append(jnp.where(odd, re, im))
+        values = first_half + second_half
         first = turned(values[:16])
         second = turned(values[16:] + [None] * (32 - len(values)))
         for g in range(16):
-            out_ref[i * 16 + g, :, :128] = first[g].astype(BF16)
-            out_ref[i * 16 + g, :, 128:] = second[g].astype(BF16)
+            out_ref[i * 16 + g, :, :128] = first[g]
+            out_ref[i * 16 + g, :, 128:] = second[g]
         return carry
 
     lax.fori_loop(0, NF // 128, tile, 0)
@@ -272,7 +287,7 @@
         gather_bins_kernel,
         in_specs=[whole] * 2,
         out_specs=whole,
-        out_shape=jax.ShapeDtypeStruct((NF // 8, channels, TILE), BF16),
+        out_shape=jax.ShapeDtypeStruct((NF // 8, channels, TILE), F32),
         compiler_params=pltpu.CompilerParams(vmem_limit_bytes=VMEM_LIMIT),
         name="gather_bins",
     )(mine, theirs)
@@ -294,19 +309,24 @@
     for copy in copies:
         copy.start()
     channels = own_ref.shape[1]
-    windows = place_ref.shape[1] // 128
     sources = 64
+    windows = place_ref.shape[1] // sources
     low = lax.broadcasted_iota(jnp.int32, (NF, 128), 1) < sources
 
     def spread(part, values, places):
-        for w in range(0, windows, 2):
-            at = places[:, w * 128 : (w + 2) * 128]
+        for begin in range(0, windows * sources, TILE):
+            at = places[:, begin : begin + TILE]
             re = jnp.dot(values[:NF], at, preferred_element_type=F32)
             im = jnp.dot(values[NF:], at, preferred_element_type=F32)
-            for e in range(2):
-                r, i = re[:, e * 128 : (e + 1) * 128], im[:, e * 128 : (e + 1) * 128]
-                src[part * windows + w + e] = jnp.where(low, r, -i)
-                src[(2 + part) * windows + w + e] = jnp.where(low, i, r)
+            for near in range(0, at.shape[1], 128):
+                r, i = re[:, near : near + 128], im[:, near : near + 128]
+                turned_r, turned_i = pltpu.roll(r, sources, 1), pltpu.roll(i, sources, 1)
+                first = part * windows + (begin + near) // sources
+                src[first] = jnp.where(low, r, -turned_i)
+                src[first + 1] = jnp.where(low, turned_r, -i)
+                second = first + 2 * windows
+                src[second] = jnp.where(low, i, turned_r)
+                src[second + 1] = jnp.where(low, turned_i, r)
 
     for part, ref in enumerate((mine_ref, theirs_ref)):
         copies[part].wait()
@@ -315,36 +335,42 @@
 
     shape = (8, TILE)
     lane = lax.broadcasted_iota(jnp.int32, shape, 1)
-    pick = (lane % 8 == lax.broadcasted_iota(jnp.int32, shape, 0)) & (lane < 32 * windows)
+    place = lax.broadcasted_iota(jnp.int32, shape, 0)
+    pick = (lane % 4 == place % 4) & (lane < 32 * windows)
+    upper = place < 4
+    early = lax.broadcasted_iota(jnp.int32, (8, 128), 0) < 4
     under = lax.broadcasted_iota(jnp.int32, (16, 128), 1) < sources
-    zeros = jnp.zeros((TILE - 32 * windows, 128), F32)
+    zeros = jnp.zeros((TILE - 32 * windows, TILE), F32)
 
     def bins(i, carry):
         pair = []
         for e in range(2):
             g = 2 * i + e
             at = pl.ds(pl.multiple_of(g * 8, 8), 8)
-            right = jnp.concatenate(
-                [src[j, at, :] for j in range(4 * windows)] + [zeros], axis=0
-            ).astype(BF16)
-            own = own_ref[g].astype(F32)
-            left = jnp.concatenate(
-                [
-                    jnp.where(pick, jnp.broadcast_to(own[c : c + 1, :], shape), 0.0)
-                    for c in range(channels)
-                ],
-                axis=0,
-            ).astype(BF16)
+            right = []
+            for j in range(4 * windows):
+                tile = src[j, at, :]
+                halves = [jnp.where(early, tile, 0.0), jnp.where(early, 0.0, tile)]
+                right.append(jnp.concatenate(halves, axis=1))
+            right = jnp.concatenate(right + [zeros], axis=0).astype(BF16)
+            left = []
+            for c in range(0, channels, 2):
+                even = jnp.broadcast_to(own_ref[g, c : c + 1, :], shape)
+                uneven = jnp.broadcast_to(own_ref[g, c + 1 : c + 2, :], shape)
+                left.append(jnp.where(pick, jnp.where(upper, even, uneven), 0.0))
+            left = jnp.concatenate(left, axis=0).astype(BF16)
             pair.append(jnp.dot(left, right, preferred_element_type=F32))
         at = pl.ds(pl.multiple_of(i * 16, 16), 16)
         at_im = pl.ds(pl.multiple_of(NF + i * 16, 16), 16)
         for c in range(0, channels, 2):
-            t = [
-                jnp.concatenate([p[(c + e) * 8 : (c + e + 1) * 8] for p in pair], axis=0)
-                for e in range(2)
-            ]
-            re = jnp.where(under, t[0], pltpu.roll(t[1], sources, 1))
-            im = jnp.where(under, pltpu.roll(t[0], sources, 1), t[1])
+            t = [[], []]
+            for p in pair:
+                first, last = p[c * 4 : c * 4 + 8, :128], p[c * 4 : c * 4 + 8, 128:]
+                t[0].append(jnp.where(early, first, pltpu.roll(last, 4, 0)))
+                t[1].append(jnp.where(early, pltpu.roll(first, 4, 0), last))
+            t = [jnp.concatenate(tiles, axis=0) for tiles in t]
+            re = jnp.where(under, t[0], t[1])
+            im = pltpu.roll(jnp.where(under, -t[1], t[0]), sources, 1)
             lanes = slice((c % 4) * 64, (c % 4) * 64 + 128)
             cross[c // 4, at, lanes] = re.astype(BF16)
             cross[c // 4, at_im, lanes] = im.astype(BF16)
@@ -379,7 +405,7 @@
 
 def correlate(own, mine, theirs, place, segs):
     groups, channels, _ = own.shape
-    windows = place.shape[1] // 128
+    windows = place.shape[1] // 64
     group = 64 // segs
     order = np.zeros((segs, 4, group, 4, segs, group), np.float32)
     for g, c, u in itertools.product(range(segs), range(4), range(group)):
@@ -397,7 +423,7 @@
             pltpu.VMEM((channels // 4, 2 * NF, TILE), BF16),
             pltpu.VMEM(mine.shape, BF16),
             pltpu.VMEM(theirs.shape, BF16),
-            pltpu.VMEM(own.shape, BF16),
+            pltpu.VMEM(own.shape, F32),
             pltpu.VMEM(table.shape, BF16),
             pltpu.SemaphoreType.DMA((4,)),
         ],
@@ -531,11 +557,11 @@
     spot_slot = jnp.sum(jnp.where(at_spot, slot[None, None, :], 0), axis=-1)
     spot_chip = jnp.sum(jnp.where(at_spot, chip[None, None, :], 0), axis=-1)
     spot_far = jnp.stack([(spot_chip[0] - my_chip) % chips, spot_chip[1]])
-    column_window = np.repeat(np.arange(per_core), 2 * spots)
+    column_window = np.repeat(np.arange(per_core), spots)
     far = np.repeat(np.arange(chips), lanes).astype(np.int32)
     placing = (
-        (jnp.tile(spot_slot, (1, 2 * per_core))[:, None, :] == np.tile(seat_slot, chips)[None, :, None])
-        & (jnp.tile(spot_far, (1, 2 * per_core))[:, None, :] == far[None, :, None])
+        (jnp.tile(spot_slot, (1, per_core))[:, None, :] == np.tile(seat_slot, chips)[None, :, None])
+        & (jnp.tile(spot_far, (1, per_core))[:, None, :] == far[None, :, None])
         & (np.tile(seat_window, chips)[:, None] == column_window[None, :])[None]
     ).astype(BF16)
 
@@ -592,10 +618,7 @@
             (jnp.tile(at, (1, per_core))[:, :, None] == row_channel[None, None, :])
             & (np.repeat(np.arange(per_core), spots)[:, None] == row_window[None, :])[None]
         ).astype(BF16)
-        spot = np.zeros((per_core, spots, per_core, 2, spots), np.float32)
-        for w in range(per_core):
-            spot[w, :, w] = np.eye(spots)[:, None, :]
-        spot = jnp.asarray(spot.reshape(per_core * spots, -1), BF16)
+        spot = jnp.eye(per_core * spots, dtype=BF16)
         first = my_core[0] == 0
         white = jnp.concatenate([jnp.where(first, own, other), jnp.where(first, other, own)])
         lags = []

time: 265 us -> 265 us (level)
    pallas_call x2, Pallas kernels: 45.9 us -> 41.2 us  [correlate(): pl.pallas_call(functools.partial(correlate_kernel, segs), in_specs=[pl.Bl...]
    pallas_call x1, Pallas kernels: 4.98 us -> 9.26 us  [gather_bins(): pl.pallas_call(gather_bins_kernel, in_specs=[whole] * 2, out_specs=whole,...]
    ppermute x3, waiting for transfers between devices: 23.4 us -> 20 us  [on_device(): up = lax.ppermute(up, 'chan', upward)]
    all_to_all x2, waiting for transfers between devices: 25.1 us -> 28.1 us  [finished(): lax.all_to_all(lag, 'seg', split_axis=0, concat_axis=0, tiled=True)]
  transfers between devices with their start and end apart: 13 -> 13, of which waited for: 11 -> 10; matrix products, arithmetic and copies ran while one was open for 5% -> 4% of each run, Pallas kernels for 19% -> 19%
where the time goes in v3:
time: 265 us
  waiting for transfers between devices  136 us (51%)
  Pallas kernels  70.4 us (27%)
  starting transfers between devices  28.7 us (11%)
  between operations  16.5 us (6%)
  other arithmetic  8.9 us (3%)
  local copies, waits for them, and re-layouts  3.69 us (1%)
    all_to_all x1, waiting for transfers between devices, on_device(): lax.all_to_all(packed, 'chan', split_axis=0, concat_axis=0, tiled=True)  67.1 us
    pallas_call x2, Pallas kernels, correlate(): pl.pallas_call(functools.partial(correlate_kernel, segs), in_specs=[pl.Bl...  41.2 us
    all_to_all x2, waiting for transfers between devices, finished(): lax.all_to_all(lag, 'seg', split_axis=0, concat_axis=0, tiled=True)  28.1 us
    ppermute x3, waiting for transfers between devices, on_device(): up = lax.ppermute(up, 'chan', upward)  20 us
    ppermute x3, waiting for transfers between devices, on_device(): down = lax.ppermute(down, 'chan', downward)  12.9 us
    pallas_call x1, Pallas kernels, transform(): pl.pallas_call(functools.partial(transform_kernel, layout), in_specs=[pl....  12 us
    pallas_call x1, Pallas kernels, gather_bins(): pl.pallas_call(gather_bins_kernel, in_specs=[whole] * 2, out_specs=whole,...  9.26 us
    ppermute x3, starting transfers between devices, on_device(): up = lax.ppermute(up, 'chan', upward)  9.13 us
  transfers between devices with their start and end apart: 13, of which 10 were waited for; matrix products, arithmetic and copies ran while one was open for 4% of the time, Pallas kernels for 19%

profile of v3, /device:TPU:0, one launch (start us, length us, event | category | flops | bytes accessed | tf_op | source)
XLA Modules:
  0.0 264.5 jit_solution(4620692568218897192)
XLA Ops:
  6.5 4.2 %pack.1 = bf16[8,2,6,32,512]{4,3,2,1,0:T(8,128)(2,1)} custom-call(s32[12]{0:T(128)} %lengths_ref.1, s32[1]{0:T(128)} %bitcast.4.start_ref, bf16[12,256,512]{2,1,0:T(8,128)(2,1)} %x_ref.1), custom_call_target="tpu_custom_call" | custom-call | tf_op jit(solution)/shard_map/pack/pallas_call | solution.py:100
  10.8 6.5 %all-to-all-start.2 = ((bf16[8,384,512]{2,1,0:T(8,128)(2,1)}), bf16[8,384,512]{2,1,0:T(8,128)(2,1)}, u32[]{:S(2)}, u32[]{:S(2)}) async-start(bf16[8,384,512]{2,1,0:T(8,128)(2,1)} %bitcast.49), calls=%async_computation.2 | async-start | bytes 6291456 | tf_op jit(solution)/shard_map/all_to_all | solution.py:519
  21.0 0.8 fusion.10.select_ref
  21.8 67.1 %all-to-all-done.2.x_ref = bf16[8,384,512]{2,1,0:T(8,128)(2,1)} async-done(((bf16[8,384,512]{2,1,0:T(8,128)(2,1)}), bf16[8,384,512]{2,1,0:T(8,128)(2,1)}, u32[]{:S(2)}, u32[]{:S(2)}) %all-to-all-start.2) | async-done | bytes 3145760 | tf_op jit(solution)/shard_map/all_to_all | solution.py:519
  88.9 12.0 %transform.1 = (bf16[192,2304]{1,0:T(8,128)(2,1)S(1)}, bf16[192,2304]{1,0:T(8,128)(2,1)S(1)}, bf16[2304,128]{1,0:T(8,128)(2,1)}, bf16[2304,128]{1,0:T(8,128)(2,1)}) custom-call(s32[1]{0:T(128)} %bitcast.3.core_ref, bf16[8,384,512]{2,1,0:T(8,128)(2,1)} %all-to-all-done.2.x_ref, bf16[9,512,512]{2,1,0:T(8,128)(2,1)} %constant.203.clone.table_hbm, ...), custom_call_target="tpu_custom_call" | custom-call | tf_op jit(solution)/shard_map/transform/pallas_call | solution.py:213
  101.0 1.3 collective-permute-start.3
  102.3 1.3 collective-permute-start.2
  103.7 11.5 %collective-permute-done.3 = bf16[2304,128]{1,0:T(8,128)(2,1)S(1)} collective-permute-done((bf16[2304,128]{1,0:T(8,128)(2,1)}, bf16[2304,128]{1,0:T(8,128)(2,1)S(1)}, u32[]{:S(2)}, u32[]{:S(2)}) %collective-permute-start.3) | collective-permute-done | bytes 589856 | tf_op jit(solution)/shard_map/ppermute | solution.py:587
  115.2 5.2 %collective-permute-start.4 = (bf16[2304,128]{1,0:T(8,128)(2,1)S(1)}, bf16[2304,128]{1,0:T(8,128)(2,1)}, u32[]{:S(2)}, u32[]{:S(2)}) collective-permute-start(bf16[2304,128]{1,0:T(8,128)(2,1)S(1)} %collective-permute-done.3), channel_id=1, source_target_pairs={{0,2},{1,3},{2,4},{3,5},{4,6},{5,7},{8,10},{9,11},{10,12},{11,13},... | collective-permute-start | bytes 1769480 | tf_op jit(solution)/shard_map/ppermute | solution.py:587
  120.4 1.3 collective-permute-start.5
  121.7 0.9 copy-done.9
  122.6 9.3 %gather_bins.1.own_hbm = f32[144,32,256]{2,1,0:T(8,128)} custom-call(bf16[6,32,2304]{2,1,0:T(8,128)(2,1)S(1)} %bitcast.48, bf16[6,32,2304]{2,1,0:T(8,128)(2,1)} %bitcast.52), custom_call_target="tpu_custom_call" | custom-call | tf_op jit(solution)/shard_map/gather_bins/pallas_call | solution.py:286
  131.9 4.8 %collective-permute-done.5 = bf16[2304,128]{1,0:T(8,128)(2,1)} collective-permute-done((bf16[2304,128]{1,0:T(8,128)(2,1)}, bf16[2304,128]{1,0:T(8,128)(2,1)}, u32[]{:S(2)}, u32[]{:S(2)}) %collective-permute-start.5) | collective-permute-done | bytes 589856 | tf_op jit(solution)/shard_map/ppermute | solution.py:588
  136.7 2.6 collective-permute-start.7
  139.3 1.5 collective-permute-start.8
  140.9 1.3 add_bitcast_fusion.1
  142.2 8.5 %collective-permute-done.7 = bf16[2304,128]{1,0:T(8,128)(2,1)S(1)} collective-permute-done((bf16[2304,128]{1,0:T(8,128)(2,1)}, bf16[2304,128]{1,0:T(8,128)(2,1)S(1)}, u32[]{:S(2)}, u32[]{:S(2)}) %collective-permute-start.7) | collective-permute-done | bytes 589856 | tf_op jit(solution)/shard_map/ppermute | solution.py:587
  150.7 1.2 add_bitcast_fusion.2
  151.8 8.0 %collective-permute-done.8 = bf16[2304,128]{1,0:T(8,128)(2,1)} collective-permute-done((bf16[2304,128]{1,0:T(8,128)(2,1)}, bf16[2304,128]{1,0:T(8,128)(2,1)}, u32[]{:S(2)}, u32[]{:S(2)}) %collective-permute-start.8) | collective-permute-done | bytes 589856 | tf_op jit(solution)/shard_map/ppermute | solution.py:588
  159.9 1.1 add_bitcast_fusion
  161.0 1.8 pad_maximum_fusion.3.mine_hbm
  163.2 1.2 copy.40
  164.8 1.0 slice_bitcast_fusion.4
  165.8 1.9 collective-permute-done.9.theirs_hbm
  167.7 20.6 %correlate.10 = bf16[4,512,512]{2,1,0:T(8,128)(2,1)} custom-call(bf16[4,2304,128]{2,1,0:T(8,128)(2,1)} %pad_maximum_fusion.3.mine_hbm, bf16[4,2304,128]{2,1,0:T(8,128)(2,1)} %collective-permute-done.9.theirs_hbm, f32[144,32,256]{2,1,0:T(8,128)} %gather_bins.1.own_hbm, bf16[512,2304]{1,0:T(8,128)(2,1)S(1)} %copy-done, ...), custom_call_target="tpu_custom_call" | custom-call | tf_op jit(solution)/shard_map/correlate/pallas_call | solution.py:416
  188.3 5.9 %all-gather.3.cloned.1.call-done = bf16[9216,128]{1,0:T(8,128)(2,1)} async-done(((bf16[2304,128]{1,0:T(8,128)(2,1)}), bf16[9216,128]{1,0:T(8,128)(2,1)}) %all-gather.3.cloned.1.call-update) | async-done | bytes 2359312 | tf_op jit(solution)/shard_map/all_gather | solution.py:592
  194.2 4.4 %all-to-all-start.3 = ((bf16[4,512,512]{2,1,0:T(8,128)(2,1)}), bf16[4,512,512]{2,1,0:T(8,128)(2,1)}, u32[]{:S(2)}, u32[]{:S(2)}) async-start(bf16[4,512,512]{2,1,0:T(8,128)(2,1)} %correlate.10), calls=%async_computation.3 | async-start | bytes 4194304 | tf_op jit(solution)/shard_map/all_to_all | solution.py:605
  199.0 20.6 %correlate.11 = bf16[4,512,512]{2,1,0:T(8,128)(2,1)} custom-call(bf16[4,2304,128]{2,1,0:T(8,128)(2,1)} %bitcast.51, bf16[4,2304,128]{2,1,0:T(8,128)(2,1)} %collective-permute-done.10.theirs_hbm, f32[144,32,256]{2,1,0:T(8,128)} %gather_bins.1.own_hbm, bf16[512,2304]{1,0:T(8,128)(2,1)S(1)} %copy-done, bf16[512,384]{1,0:T(8,128)(2,1)} %get-tuple-element.425.place_ref, ...), custom_call_target="tpu_custom_call" | custom-call | tf_op jit(solution)/shard_map/correlate/pallas_call | solution.py:416
  219.7 4.8 %all-to-all-done.3.refs_0_ = bf16[4,512,512]{2,1,0:T(8,128)(2,1)} async-done(((bf16[4,512,512]{2,1,0:T(8,128)(2,1)}), bf16[4,512,512]{2,1,0:T(8,128)(2,1)}, u32[]{:S(2)}, u32[]{:S(2)}) %all-to-all-start.3) | async-done | bytes 2097184 | tf_op jit(solution)/shard_map/all_to_all | solution.py:605
  224.5 4.5 %all-to-all-start.4 = ((bf16[4,512,512]{2,1,0:T(8,128)(2,1)}), bf16[4,512,512]{2,1,0:T(8,128)(2,1)}, u32[]{:S(2)}, u32[]{:S(2)}) async-start(bf16[4,512,512]{2,1,0:T(8,128)(2,1)} %correlate.11), calls=%async_computation.4 | async-start | bytes 4194304 | tf_op jit(solution)/shard_map/all_to_all | solution.py:605
  230.7 23.3 %all-to-all-done.4.refs_1_ = bf16[4,512,512]{2,1,0:T(8,128)(2,1)} async-done(((bf16[4,512,512]{2,1,0:T(8,128)(2,1)}), bf16[4,512,512]{2,1,0:T(8,128)(2,1)}, u32[]{:S(2)}, u32[]{:S(2)}) %all-to-all-start.4) | async-done | bytes 2097184 | tf_op jit(solution)/shard_map/all_to_all | solution.py:605
  254.0 3.6 %finish.5 = f32[32,32,512]{2,1,0:T(8,128)} custom-call(bf16[64,256]{1,0:T(8,128)(2,1)} %and_convert_fusion.2.place_ref, bf16[4,512,512]{2,1,0:T(8,128)(2,1)} %all-to-all-done.3.refs_0_, bf16[4,512,512]{2,1,0:T(8,128)(2,1)} %all-to-all-done.4.refs_1_), custom_call_target="tpu_custom_call" | custom-call | tf_op jit(solution)/shard_map/finish/pallas_call | solution.py:453
  (80 shorter events, 4.0 us)
Async XLA Ops:
  10.8 6.6 %copy-start.38 = (s32[128]{0:T(128)S(1)}, s32[128]{0:T(128)}, u32[]{:S(2)}) copy-start(s32[128]{0:T(128)} %param.32) | copy-start | bytes 1540
  10.8 6.8 %copy-start.34 = (s32[8,128]{1,0:T(8,128)S(1)}, s32[8,128]{1,0:T(8,128)}, u32[]{:S(2)}) copy-start(s32[8,128]{1,0:T(8,128)} %constant.193.clone) | copy-start | bytes 12292
  10.8 9.0 %copy-start.19 = (pred[128,384]{1,0:T(32,128)(4,1)S(1)}, pred[128,384]{1,0:T(32,128)(4,1)}, u32[]{:S(2)}) copy-start(pred[128,384]{1,0:T(32,128)(4,1)} %constant.215) | copy-start | bytes 147460
  10.8 10.0 %copy-start.37 = (s32[128]{0:T(128)S(1)}, s32[128]{0:T(128)}, u32[]{:S(2)}) copy-start(s32[128]{0:T(128)} %constant.213) | copy-start | bytes 1540
  10.8 10.2 %copy-start.17 = (s32[384]{0:T(512)S(1)}, s32[384]{0:T(512)}, u32[]{:S(2)}) copy-start(s32[384]{0:T(512)} %constant.214) | copy-start | bytes 4612
  10.8 78.1 %all-to-all-start.2 = ((bf16[8,384,512]{2,1,0:T(8,128)(2,1)}), bf16[8,384,512]{2,1,0:T(8,128)(2,1)}, u32[]{:S(2)}, u32[]{:S(2)}) async-start(bf16[8,384,512]{2,1,0:T(8,128)(2,1)} %bitcast.49), calls=%async_computation.2 | async-start | bytes 6291456 | tf_op jit(solution)/shard_map/all_to_all | solution.py:519
  17.3 176.9 %all-gather.3.cloned.1.call-start = ((), (), s32[]{:S(2)}) async-start(), calls=%async_computation.5 | async-start | bytes 2949120 | tf_op jit(solution)/shard_map/all_gather | solution.py:592
  100.9 30.9 %copy-start.4 = (bf16[192,2304]{1,0:T(8,128)(2,1)}, bf16[192,2304]{1,0:T(8,128)(2,1)S(1)}, u32[]{:S(2)}) copy-start(bf16[192,2304]{1,0:T(8,128)(2,1)S(1)} %get-tuple-element.540) | copy-start | bytes 2654212
  101.0 14.3 %collective-permute-start.3 = (bf16[2304,128]{1,0:T(8,128)(2,1)}, bf16[2304,128]{1,0:T(8,128)(2,1)S(1)}, u32[]{:S(2)}, u32[]{:S(2)}) collective-permute-start(bf16[2304,128]{1,0:T(8,128)(2,1)} %get-tuple-element.239), channel_id=1, source_target_pairs={{0,2},{1,3},{2,4},{3,5},{4,6},{5,7},{8,10},{9,11},{10,12},{11,13},... | collective-permute-start | bytes 1769480 | tf_op jit(solution)/shard_map/ppermute | solution.py:587
  102.3 18.1 %collective-permute-start.2 = (bf16[2304,128]{1,0:T(8,128)(2,1)}, bf16[2304,128]{1,0:T(8,128)(2,1)}, u32[]{:S(2)}, u32[]{:S(2)}) collective-permute-start(bf16[2304,128]{1,0:T(8,128)(2,1)} %get-tuple-element.239), channel_id=1, source_target_pairs={{2,0},{3,1},{4,2},{5,3},{6,4},{7,5},{10,8},{11,9},{12,10},{13,11},... | collective-permute-start | bytes 1769480 | tf_op jit(solution)/shard_map/ppermute | solution.py:588
  103.6 18.1 %collective-permute-start.6 = (bf16[192,2304]{1,0:T(8,128)(2,1)S(1)}, bf16[192,2304]{1,0:T(8,128)(2,1)S(1)}, u32[]{:S(2)}, u32[]{:S(2)}) collective-permute-start(bf16[192,2304]{1,0:T(8,128)(2,1)S(1)} %get-tuple-element.540), channel_id=1, source_target_pairs={{0,1},{1,0},{2,3},{3,2},{4,5},{5,4},{6,7},{7,6},{8,9},{9,8},{10,11... | collective-permute-start | bytes 2654216 | tf_op jit(solution)/shard_map/ppermute | solution.py:580
  115.2 25.6 %copy-start.11 = (bf16[2304,128]{1,0:T(8,128)(2,1)}, bf16[2304,128]{1,0:T(8,128)(2,1)S(1)}, u32[]{:S(2)}) copy-start(bf16[2304,128]{1,0:T(8,128)(2,1)S(1)} %collective-permute-done.3) | copy-start | bytes 1769476
  115.2 16.6 %collective-permute-start.4 = (bf16[2304,128]{1,0:T(8,128)(2,1)S(1)}, bf16[2304,128]{1,0:T(8,128)(2,1)}, u32[]{:S(2)}, u32[]{:S(2)}) collective-permute-start(bf16[2304,128]{1,0:T(8,128)(2,1)S(1)} %collective-permute-done.3), channel_id=1, source_target_pairs={{0,2},{1,3},{2,4},{3,5},{4,6},{5,7},{8,10},{9,11},{10,12},{11,13},... | collective-permute-start | bytes 1769480 | tf_op jit(solution)/shard_map/ppermute | solution.py:587
  120.4 16.3 %collective-permute-start.5 = (bf16[2304,128]{1,0:T(8,128)(2,1)}, bf16[2304,128]{1,0:T(8,128)(2,1)}, u32[]{:S(2)}, u32[]{:S(2)}) collective-permute-start(bf16[2304,128]{1,0:T(8,128)(2,1)} %collective-permute-done.2), channel_id=1, source_target_pairs={{2,0},{3,1},{4,2},{5,3},{6,4},{7,5},{10,8},{11,9},{12,10},{13,11},... | collective-permute-start | bytes 1769480 | tf_op jit(solution)/shard_map/ppermute | solution.py:588
  121.7 0.9 copy-start.9
  136.7 14.0 %collective-permute-start.7 = (bf16[2304,128]{1,0:T(8,128)(2,1)}, bf16[2304,128]{1,0:T(8,128)(2,1)S(1)}, u32[]{:S(2)}, u32[]{:S(2)}) collective-permute-start(bf16[2304,128]{1,0:T(8,128)(2,1)} %collective-permute-done.4), channel_id=1, source_target_pairs={{0,2},{1,3},{2,4},{3,5},{4,6},{5,7},{8,10},{9,11},{10,12},{11,13},... | collective-permute-start | bytes 1769480 | tf_op jit(solution)/shard_map/ppermute | solution.py:587
  139.3 20.5 %collective-permute-start.8 = (bf16[2304,128]{1,0:T(8,128)(2,1)}, bf16[2304,128]{1,0:T(8,128)(2,1)}, u32[]{:S(2)}, u32[]{:S(2)}) collective-permute-start(bf16[2304,128]{1,0:T(8,128)(2,1)} %collective-permute-done.5), channel_id=1, source_target_pairs={{2,0},{3,1},{4,2},{5,3},{6,4},{7,5},{10,8},{11,9},{12,10},{13,11},... | collective-permute-start | bytes 1769480 | tf_op jit(solution)/shard_map/ppermute | solution.py:588
  142.2 17.7 %copy-start.12 = (bf16[2304,128]{1,0:T(8,128)(2,1)S(1)}, bf16[2304,128]{1,0:T(8,128)(2,1)}, u32[]{:S(2)}) copy-start(bf16[2304,128]{1,0:T(8,128)(2,1)} %copy-done.11) | copy-start | bytes 1769476
  142.2 18.8 %copy-start.10 = (bf16[2304,128]{1,0:T(8,128)(2,1)S(1)}, bf16[2304,128]{1,0:T(8,128)(2,1)}, u32[]{:S(2)}) copy-start(bf16[2304,128]{1,0:T(8,128)(2,1)} %get-tuple-element.239) | copy-start | bytes 1769476
  161.0 3.4 %copy-start.35 = (s32[512]{0:T(512)S(1)}, s32[512]{0:T(512)}, u32[]{:S(2)}) copy-start(s32[512]{0:T(512)} %constant.216) | copy-start | bytes 6148
  161.0 3.4 %copy-start.36 = (s32[512]{0:T(512)S(1)}, s32[512]{0:T(512)}, u32[]{:S(2)}) copy-start(s32[512]{0:T(512)} %constant.217) | copy-start | bytes 6148
  162.8 4.9 %copy-start = (bf16[512,2304]{1,0:T(8,128)(2,1)S(1)}, bf16[512,2304]{1,0:T(8,128)(2,1)}, u32[]{:S(2)}) copy-start(bf16[512,2304]{1,0:T(8,128)(2,1)} %constant.208.clone.table_hbm) | copy-start | bytes 7077892
  162.8 4.9 %copy-start.5 = (bf16[256,256]{1,0:T(8,128)(2,1)S(1)}, bf16[256,256]{1,0:T(8,128)(2,1)}, u32[]{:S(2)}) copy-start(bf16[256,256]{1,0:T(8,128)(2,1)} %constant.209.clone.order_ref) | copy-start | bytes 393220
  162.8 4.9 %collective-permute-start.9 = (bf16[4,2304,128]{2,1,0:T(8,128)(2,1)}, bf16[4,2304,128]{2,1,0:T(8,128)(2,1)}, u32[]{:S(2)}, u32[]{:S(2)}) collective-permute-start(bf16[4,2304,128]{2,1,0:T(8,128)(2,1)} %pad_maximum_fusion.3.mine_hbm), channel_id=1, source_target_pairs={{0,1},{1,0},{2,3},{3,2},{4,5},{5,4},{6,7},{7,6},{8,9},{9,8},{10,11... | collective-permute-start | bytes 7077896 | tf_op jit(solution)/shard_map/ppermute | solution.py:598
  194.2 4.9 %collective-permute-start.10 = (bf16[4,2304,128]{2,1,0:T(8,128)(2,1)}, bf16[4,2304,128]{2,1,0:T(8,128)(2,1)}, u32[]{:S(2)}, u32[]{:S(2)}) collective-permute-start(bf16[4,2304,128]{2,1,0:T(8,128)(2,1)} %bitcast.50), channel_id=1, source_target_pairs={{0,1},{1,0},{2,3},{3,2},{4,5},{5,4},{6,7},{7,6},{8,9},{9,8},{10,11... | collective-permute-start | bytes 7077896 | tf_op jit(solution)/shard_map/ppermute | solution.py:598
  194.2 30.3 %all-to-all-start.3 = ((bf16[4,512,512]{2,1,0:T(8,128)(2,1)}), bf16[4,512,512]{2,1,0:T(8,128)(2,1)}, u32[]{:S(2)}, u32[]{:S(2)}) async-start(bf16[4,512,512]{2,1,0:T(8,128)(2,1)} %correlate.10), calls=%async_computation.3 | async-start | bytes 4194304 | tf_op jit(solution)/shard_map/all_to_all | solution.py:605
  219.7 10.3 %copy-start.13 = (pred[64,256]{1,0:T(32,128)(4,1)S(1)}, pred[64,256]{1,0:T(32,128)(4,1)}, u32[]{:S(2)}) copy-start(pred[64,256]{1,0:T(32,128)(4,1)} %constant.202.clone) | copy-start | bytes 49156
  219.7 10.3 %copy-start.20 = (s32[256]{0:T(256)S(1)}, s32[256]{0:T(256)}, u32[]{:S(2)}) copy-start(s32[256]{0:T(256)} %constant.211) | copy-start | bytes 3076
  219.7 10.3 %copy-start.22 = (s32[256]{0:T(256)S(1)}, s32[256]{0:T(256)}, u32[]{:S(2)}) copy-start(s32[256]{0:T(256)} %constant.212) | copy-start | bytes 3076
  224.5 29.6 %all-to-all-start.4 = ((bf16[4,512,512]{2,1,0:T(8,128)(2,1)}), bf16[4,512,512]{2,1,0:T(8,128)(2,1)}, u32[]{:S(2)}, u32[]{:S(2)}) async-start(bf16[4,512,512]{2,1,0:T(8,128)(2,1)} %correlate.11), calls=%async_computation.4 | async-start | bytes 4194304 | tf_op jit(solution)/shard_map/all_to_all | solution.py:605
  229.2 0.8 copy-start.28
  230.7 26.9 %copy-start.7 = (pred[384,384]{1,0:T(32,128)(4,1)S(1)}, pred[384,384]{1,0:T(32,128)(4,1)}, u32[]{:S(2)}) copy-start(pred[384,384]{1,0:T(32,128)(4,1)} %constant.278) | copy-start | bytes 442372
  (1 other events, 0.7 us)
Sparse Core Ops, SparseCore 0:
  141.0 53.1 all-gather.2
